TPU v7x, 32 devices: a whole 2x2x4 slice. The times are simulated.
32 devices in a mesh: row: 8 (over z, y), col: 4 (over x, core).
Axes of the slice: x: 2, y: 2, z: 4, core: 2. Of those that a mesh axis runs over, the one named last changes fastest.
Arguments:
- amplitudes: float32 [16, 16, 25600], P('row', 'col'), as said below
- cycle_int: float32 [16, 16, 25600], P('row', 'col'), as said below
- ladder_int: float32 [4, 1600, 6400], P(None, 'col'), may hold values from -0.078125 to 0.078125
- window: int32 [4, 2], replicated, may hold values from 0 to 3, as said below
Outputs:
- residual: float32 [16, 16, 25600], P('row', 'col')
Inputs may be any that keep to these rules, and one draw needn't show every extreme that they name: amplitudes[i,j,a*160+b] == amplitudes[j,i,b*160+a]. cycle_int[k,j,c*160+b] == cycle_int[j,k,b*160+c]. `window`: the 4 pairs are distinct.
All inputs are finite; a program needn't handle non-finite values.
Results may differ from a plain program's by a relative error of at most 0.0001.
Values sent between devices are 32-bit elements; how exact they have to be, the bound alone decides.
No kernel may reach another device: no remote copies, remote signals or barrier semaphores. Data moves between devices by JAX's collectives and lax.ppermute only.
A program may use at most 320 MiB of HBM per device.

v0:
```python
import functools

import jax
import jax.numpy as jnp
from jax import lax
from jax.experimental import pallas as pl
from jax.experimental.pallas import tpu as pltpu
from jax.sharding import PartitionSpec as P

NIRR = 4
VI = 40
NWIN = 4
AXES = ("row", "col")


def cost(us):
    return pl.CostEstimate(flops=int(us * 1e9), bytes_accessed=int(us * 3e6), transcendentals=0)


def general(amplitudes, cycle_int, ladder_int, window):
    highest = lax.Precision.HIGHEST
    rows_i, cols_j, flat_pairs = amplitudes.shape
    virtual = NIRR * VI
    sector = VI
    by_rows = lax.all_gather(amplitudes, "col", axis=1, tiled=True)
    total_j = by_rows.shape[1]
    rows_four = by_rows.reshape(rows_i, total_j, virtual, virtual)
    cycle_down = lax.all_gather(cycle_int, "row", axis=0, tiled=True)
    cycle_across = lax.all_gather(cycle_int, "col", axis=1, tiled=True)
    down_four = cycle_down.reshape(cycle_down.shape[0], cols_j, virtual, virtual)
    direct = 2.0 * jnp.einsum(
        "ikac,kjcb->ijab", rows_four, down_four, precision=highest
    ) - jnp.einsum("ikca,kjcb->ijab", rows_four, down_four, precision=highest)
    by_cols = lax.all_gather(amplitudes, "row", axis=0, tiled=True)
    cols_four = by_cols.reshape(by_cols.shape[0], cols_j, virtual, virtual)
    across_four = cycle_across.reshape(rows_i, cycle_across.shape[1], virtual, virtual)
    mirror = 2.0 * jnp.einsum(
        "kjcb,ikac->ijab", cols_four, across_four, precision=highest
    ) - jnp.einsum("kjbc,ikac->ijab", cols_four, across_four, precision=highest)
    zero = jnp.int32(0)
    pair_cols = ladder_int.shape[1]
    blocks_out = []
    for which in range(NWIN):
        first = window[which, 0]
        second = window[which, 1]
        summed = jnp.zeros((rows_i, total_j, pair_cols), jnp.float32)
        for irrep in range(NIRR):
            other = jnp.bitwise_xor(jnp.bitwise_xor(first, second), jnp.int32(irrep))
            block_in = lax.dynamic_slice(
                rows_four,
                (zero, zero, jnp.int32(irrep * sector), other * sector),
                (rows_i, total_j, sector, sector),
            )
            weights = ladder_int[
                which, :, irrep * sector * sector : (irrep + 1) * sector * sector
            ].reshape(pair_cols, sector, sector)
            summed = summed + lax.dot_general(
                block_in,
                weights,
                (((2, 3), (1, 2)), ((), ())),
                precision=highest,
                preferred_element_type=jnp.float32,
            )
        blocks_out.append(summed)
    stacked = jnp.stack(blocks_out, 2)
    returned = lax.all_to_all(stacked, "col", split_axis=1, concat_axis=3, tiled=True)
    ladder = place_ladder(returned, window)
    return (ladder + direct + mirror).reshape(rows_i, cols_j, virtual * virtual)


def place_ladder(returned, window):
    rows_i, cols_j = returned.shape[:2]
    virtual = NIRR * VI
    ladder = jnp.zeros((rows_i, cols_j, virtual, virtual), jnp.float32)
    for which in range(NWIN):
        placed = returned[:, :, which].reshape(rows_i, cols_j, VI, VI)
        ladder = lax.dynamic_update_slice(
            ladder, placed, (0, 0, window[which, 0] * VI, window[which, 1] * VI)
        )
    return ladder


def split(x):
    high = x.astype(jnp.bfloat16)
    low = (x - high.astype(jnp.float32)).astype(jnp.bfloat16)
    return high, low


def dot(a, b):
    return jnp.dot(a, b, preferred_element_type=jnp.float32)


def dot_t(a, b):
    return lax.dot_general(a, b, (((1,), (1,)), ((), ())), preferred_element_type=jnp.float32)


def ladder_kernel(info, *refs):
    kinds, w_ref, out_ref, both = refs[:-3], refs[-3], refs[-2], refs[-1]
    rows = kinds[0].shape[1]
    count = rows * len(kinds)

    @pl.when(pl.program_id(1) == 0)
    def _():
        high, low = split(jnp.concatenate([k[0] for k in kinds], axis=0))
        both[0:count, :] = high
        both[count:, :] = low

    high, low = split(w_ref[0])
    wide = dot_t(high, both[...])
    out_ref[0, 0] = (wide[:, :count] + wide[:, count:] + dot_t(low, both[0:count, :])).T


def ladder_part(kinds, ladder_int, window, begin, count):
    _, rows, depth = kinds[0].shape
    total = rows * len(kinds)
    pairs = ladder_int.shape[1]
    step = pairs // 2
    return pl.pallas_call(
        ladder_kernel,
        out_shape=jax.ShapeDtypeStruct((count, pairs // step, total, step), jnp.float32),
        grid_spec=pltpu.PrefetchScalarGridSpec(
            num_scalar_prefetch=1,
            grid=(count, pairs // step),
            in_specs=[pl.BlockSpec((1, rows, depth), lambda w, n, s: (jnp.bitwise_xor(s[w + begin, 0], s[w + begin, 1]), 0, 0))] * len(kinds)
            + [pl.BlockSpec((1, step, depth), lambda w, n, s: (w + begin, n, 0))],
            out_specs=pl.BlockSpec((1, 1, total, step), lambda w, n, s: (w, n, 0, 0)),
            scratch_shapes=[pltpu.VMEM((2 * total, depth), jnp.bfloat16)],
        ),
        compiler_params=pltpu.CompilerParams(vmem_limit_bytes=32 * 2**20),
        cost_estimate=cost(5.5 * count),
        name="ladder",
    )(window, *kinds, ladder_int)


def whole(kernel, name, us, shapes, args, info=None, dtype=jnp.float32):
    def spec(shape):
        return pl.BlockSpec(tuple(shape), lambda g: (0,) * len(shape))

    specs = [spec(a.shape) for a in args]
    if info is not None:
        specs = [pl.BlockSpec(memory_space=pltpu.SMEM)] + specs
        args = (info, *args)
    return pl.pallas_call(
        kernel,
        out_shape=[jax.ShapeDtypeStruct(shape, dtype) for shape in shapes],
        grid=(1,),
        in_specs=specs,
        out_specs=[spec(shape) for shape in shapes],
        compiler_params=pltpu.CompilerParams(vmem_limit_bytes=32 * 2**20),
        cost_estimate=cost(us),
        name=name,
    )(*args)


def place():
    row, col = lax.axis_index("row"), lax.axis_index("col")
    return row // 2, row % 2, col


def sort_kernel(flat_ref, out_ref):
    rows_i, cols_j, flat = flat_ref.shape
    group = 4 * NIRR * VI
    for g in range(flat // group):
        x = flat_ref[:, :, g * group : (g + 1) * group].reshape(rows_i * cols_j, group)
        for d in range(NIRR):
            line = [x[:, (a * NIRR + d) * VI : (a * NIRR + d + 1) * VI] for a in range(4)]
            kind = (g * 4 // VI) ^ d
            out_ref[kind, :, g * 4 * VI : (g + 1) * 4 * VI] = jnp.concatenate(line, axis=1)


def turn_kernel(four_ref, zero_ref, one_ref):
    rows_i, cols_j, v, _ = four_ref.shape
    for g, out_ref in enumerate((zero_ref, one_ref)):
        out_ref[...] = jnp.concatenate(
            [four_ref[k, 2 * h + g].T for h in range(2) for k in range(rows_i)], axis=1
        )


def pair_kernel(four_ref, keep_ref, give_ref):
    rows_i, cols_j, v, _ = four_ref.shape
    halves = []
    for h in range(2):
        line = []
        for k in range(2):
            for i in range(rows_i):
                block = four_ref[i, 2 * h + k]
                line.append(2.0 * block.T - block)
        halves.append(jnp.concatenate(line, axis=1))
    low = place()[1] == 0
    keep_ref[...] = jnp.where(low, halves[0], halves[1])
    give_ref[...] = jnp.where(low, halves[1], halves[0])


def join_kernel(keep_ref, got_ref, out_ref):
    v = keep_ref.shape[0]
    n = keep_ref.shape[1] // 2
    low = place()[1] == 0
    for k in range(2):
        keep, got = keep_ref[:, k * n : (k + 1) * n], got_ref[:, k * n : (k + 1) * n]
        out_ref[k * v : (k + 1) * v, :] = jnp.concatenate(
            [jnp.where(low, keep, got), jnp.where(low, got, keep)], axis=1
        )


def arrange_kernel(*refs):
    sources, (high_ref, low_ref) = refs[:4], refs[4:]
    col = place()[2]
    for rel in range(4):
        at = jnp.bitwise_xor(col, rel)
        high_ref[at], low_ref[at] = split(sources[rel][...])


def cycle_kernel(planes, has_acc, final, *refs):
    refs = list(refs)
    high_ref, low_ref = refs.pop(0), refs.pop(0)
    total = refs.pop(0)[...] if has_acc else None
    z, y, _ = place()
    for plane in planes:
        x = refs.pop(0)[...]
        if plane in ("two", "three"):
            x = jnp.where(z < 2, x, refs.pop(0)[...])
        n = x.shape[1] // 2
        m = 2 * x.shape[0]
        high, low = split(jnp.concatenate([x[:, :n], x[:, n:]], axis=0))
        at = {
            "own": z,
            "below": jnp.maximum(z - 1, 0),
            "above": jnp.minimum(z + 1, 3),
            "two": jnp.bitwise_xor(z, 2),
            "three": 3 - z,
        }[plane]
        u_high, u_low = high_ref[at], low_ref[at]
        wide = dot(jnp.concatenate([high, low], axis=0), u_high)
        part = wide[:m] + wide[m:] + dot(high, u_low)
        total = part if total is None else total + part
    if not final:
        refs.pop(0)[...] = total
        return
    keep_ref, give_ref = refs
    v = total.shape[0] // 2
    n = total.shape[1] // 2
    sides = [
        jnp.concatenate([total[h * v : (h + 1) * v, r * n : (r + 1) * n] for h in range(2)], axis=1)
        for r in range(2)
    ]
    low = y == 0
    keep_ref[...] = jnp.where(low, sides[0], sides[1])
    give_ref[...] = jnp.where(low, sides[1], sides[0])


def cycle_part(high, low, chunks, acc, final):
    args = [high, low] + ([] if acc is None else [acc]) + [x for c in chunks for x in c[1]]
    v, n = chunks[0][1][0].shape
    shapes = [(v, n)] * 2 if final else [(2 * v, n)]
    kernel = functools.partial(cycle_kernel, tuple(c[0] for c in chunks), acc is not None, final)
    return whole(kernel, "cycle", 1 + 1.2 * len(chunks), shapes, args)


def add_kernel(keep_ref, got_ref, total_ref, same_ref, cross_ref):
    total = keep_ref[...] + got_ref[...]
    total_ref[...] = total
    n = total.shape[1] // 2
    low = place()[1] == 0
    same_ref[...] = jnp.where(low, total[:, :n], total[:, n:])
    cross_ref[...] = jnp.where(low, total[:, n:], total[:, :n])


def merge_kernel(window, zero_ref, one_ref, s0_ref, c0_ref, s1_ref, c1_ref, early_ref, late_ref, out_ref):
    rows_i, cols_j, v, _ = out_ref.shape
    low = place()[1] == 0
    totals = zero_ref, one_ref
    for i, (s_ref, c_ref) in enumerate(((s0_ref, c0_ref), (s1_ref, c1_ref))):
        same, cross = s_ref[...], c_ref[...]
        image = jnp.where(low, same, cross), jnp.where(low, cross, same)
        for j in range(cols_j):
            at = ((j // 2) * 2 + i) * v
            turned = totals[j % 2][:, at : at + v].T
            to = (j % 2) * v
            out_ref[i, j] = turned + image[j // 2][:, to : to + v]
    for which in range(NWIN):
        source = (early_ref, late_ref)[which // 2]
        first, second = window[which, 0], window[which, 1]
        rows = pl.ds(pl.multiple_of(first * VI, 8), VI)
        for i in range(rows_i):
            for j in range(cols_j):
                piece = source[which % 2, i, j]
                wide = jnp.concatenate(
                    [jnp.where(second == q, piece, 0.0) for q in range(NIRR)], axis=1
                )
                out_ref[i, j, rows, :] += wide


def permutation(rule):
    pairs = []
    for dev in range(32):
        row, col = divmod(dev, 4)
        to = rule(row // 2, row % 2, col // 2, col % 2)
        if to is not None and 0 <= to[0] < 4:
            pairs.append((dev, (to[0] * 2 + to[1]) * 4 + to[2] * 2 + to[3]))
    return pairs


def blocked(amplitudes, cycle_int, ladder_int, window):
    rows_i, cols_j, flat = amplitudes.shape
    v = NIRR * VI
    col = lax.axis_index("col")
    x, core = col // 2, col % 2
    four = (rows_i, cols_j, v, v)
    slab = (v, cols_j * v)

    def send(a, rule):
        names.append(str(len(names)))
        with jax.named_scope("send" + names[-1]):
            return lax.ppermute(a, AXES, permutation(rule))

    swap = lambda a: send(a, lambda z, y, x, k: (z, y, x, 1 - k))
    swap_x = lambda a: send(a, lambda z, y, x, k: (z, y, 1 - x, k))
    swap_xk = lambda a: send(a, lambda z, y, x, k: (z, y, 1 - x, 1 - k))
    swap_y = lambda a: send(a, lambda z, y, x, k: (z, 1 - y, x, k))
    up = lambda a: send(a, lambda z, y, x, k: (z + 1, y, x, k))
    down = lambda a: send(a, lambda z, y, x, k: (z - 1, y, x, k))
    image = lambda a: send(a, lambda z, y, x, k: (2 * x + k, y, z // 2, z % 2))
    image_y = lambda a: send(a, lambda z, y, x, k: (2 * x + k, 1 - y, z // 2, z % 2))
    names = []
    after = lax.optimization_barrier

    def returned(laddered):
        part = lambda n: laddered[:, :, 8 * n : 8 * n + 8]
        got = jnp.stack([part(0), swap(part(1)), swap_x(part(2)), swap_xk(part(3))])
        got = jnp.where(core == 0, got, jnp.stack([got[1], got[0], got[3], got[2]]))
        got = jnp.where(x == 0, got, jnp.concatenate([got[2:], got[:2]]))
        count = laddered.shape[0]
        return jnp.transpose(got, (1, 3, 0, 2, 4)).reshape(count, rows_i, cols_j, VI, VI)

    def products(own, a1, b1, a2, b2):
        return [("own", [own]), ("below", [a1]), ("above", [b1]), ("two", [b2, a2])]

    def add(keep, got):
        return whole(add_kernel, "add", 1, [slab] + [(v, slab[1] // 2)] * 2, (keep, got))

    x0, x1 = whole(turn_kernel, "turn", 1.5, [slab] * 2, (cycle_int.reshape(four),))
    a10, b10 = up(x0), down(x0)
    a11, b11 = up(x1), down(x1)
    amplitudes, x0, x1 = after((amplitudes, x0, x1))
    keep, give = whole(pair_kernel, "pair", 1.5, [slab] * 2, (amplitudes.reshape(four),))
    got = swap_y(give)
    a10, b10, keep, amplitudes = after((a10, b10, keep, amplitudes))

    a20, b20 = up(a10), down(b10)
    (kinds,) = whole(
        sort_kernel, "sort", 8, [(NIRR, rows_i * cols_j, flat // NIRR)], (amplitudes,)
    )
    a11, b11, got, kinds = after((a11, b11, got, kinds))

    a21, b21 = up(a11), down(b11)
    (u,) = whole(join_kernel, "join", 1, [(rows_i * v, cols_j * v)], (keep, got))
    u_x, u_k = swap_x(u), swap(u)
    a20, b20, u, u_k, kinds = after((a20, b20, u, u_k, kinds))

    a30, b30 = up(a20), down(b20)
    kinds_k = swap(kinds)
    a21, b21, u_x, kinds, kinds_k = after((a21, b21, u_x, kinds, kinds_k))

    a31, b31 = up(a21), down(b21)
    u_xk, kinds_x = swap(u_x), swap_x(kinds)
    high, low = whole(
        arrange_kernel,
        "arrange",
        3,
        [(4, rows_i * v, cols_j * v)] * 2,
        (u, u_k, u_x, u_xk),
        None,
        jnp.bfloat16,
    )
    a30, b30, high, low = after((a30, b30, high, low))

    keep0, give0 = cycle_part(
        high, low, products(x0, a10, b10, a20, b20) + [("three", [b30, a30])], None, True
    )
    high, low, give0 = after((high, low, give0))
    got0 = swap_y(give0)
    (part,) = cycle_part(high, low, products(x1, a11, b11, a21, b21), None, False)
    a31, b31, part, kinds_x = after((a31, b31, part, kinds_x))

    keep1, give1 = cycle_part(high, low, [("three", [b31, a31])], part, True)
    kinds_xk = swap(kinds_x)
    give1, kinds_xk, got0 = after((give1, kinds_xk, got0))
    got1 = swap_y(give1)
    total0, same0, cross0 = add(keep0, got0)
    all_kinds, total0, same0, cross0 = after(((kinds, kinds_k, kinds_x, kinds_xk), total0, same0, cross0))
    same0, cross0 = image(same0), image_y(cross0)
    early = ladder_part(all_kinds, ladder_int, window, 0, 2)
    got1, early, all_kinds = after((got1, early, all_kinds))

    total1, same1, cross1 = add(keep1, got1)
    same1, cross1, total1, all_kinds = after((same1, cross1, total1, all_kinds))
    same1, cross1 = image(same1), image_y(cross1)
    late = ladder_part(all_kinds, ladder_int, window, 2, 2)
    same0, cross0, late = after((same0, cross0, late))
    both = returned(jnp.concatenate([early, late]))
    (merged,) = whole(
        merge_kernel,
        "merge",
        2,
        [four],
        (total0, total1, same0, cross0, same1, cross1, both[:2], both[2:]),
        window,
    )
    return merged.reshape(rows_i, cols_j, flat)


def solution(mesh):
    placed = (P("row", "col", None), P("row", "col", None), P(None, "col", None), P())

    def on_device(amplitudes, cycle_int, ladder_int, window):
        fits = mesh.shape["row"] == 8 and mesh.shape["col"] == 4
        body = blocked if fits and amplitudes.shape[:2] == (2, 4) else general
        return body(amplitudes, cycle_int, ladder_int, window)

    return jax.shard_map(
        on_device, mesh=mesh, in_specs=placed, out_specs=P("row", "col", None), check_vma=False
    )
```

profile of v0, /device:TPU:2, one launch (start us, length us, event | category | flops | bytes accessed | tf_op | source)
XLA Modules:
  0.0 169.5 jit_solution(7956188632357162197)
XLA Ops:
  0.0 2.0 %reshape.12.four_ref = f32[2,4,160,160]{3,2,1,0:T(8,128)S(1)} reshape(f32[2,4,25600]{2,1,0:T(4,128)} %param.5) | data formatting | bytes 1638400 | tf_op jit(solution)/shard_map/reshape | solution.py:341
  2.0 0.8 turn.1
  2.8 4.3 %collective-permute-start.3 = (f32[160,640]{1,0:T(8,128)S(1)}, f32[160,640]{1,0:T(8,128)}, u32[]{:S(2)}, u32[]{:S(2)}) collective-permute-start(f32[160,640]{1,0:T(8,128)S(1)} %get-tuple-element.106.refs_2_), channel_id=1, source_target_pairs={{0,8},{1,9},{2,10},{3,11},{4,12},{5,13},{6,14},{7,15},{8,16},{9,17... | collective-permute-start | bytes 1228808 | tf_op jit(solution)/shard_map/send0/ppermute | solution.py:314
  7.0 1.3 collective-permute-start.4
  8.3 5.3 %collective-permute-start = (f32[160,640]{1,0:T(8,128)S(1)}, f32[160,640]{1,0:T(8,128)}, u32[]{:S(2)}, u32[]{:S(2)}) collective-permute-start(f32[160,640]{1,0:T(8,128)S(1)} %get-tuple-element.112.refs_2_), channel_id=1, source_target_pairs={{0,8},{1,9},{2,10},{3,11},{4,12},{5,13},{6,14},{7,15},{8,16},{9,17... | collective-permute-start | bytes 1228808 | tf_op jit(solution)/shard_map/send2/ppermute | solution.py:314
  13.6 1.3 collective-permute-start.1
  14.9 0.8 reshape.13.four_ref
  15.7 0.8 pair.1
  16.5 1.6 collective-permute-start.2
  18.1 3.3 %collective-permute-done.4.refs_4_ = f32[160,640]{1,0:T(8,128)} collective-permute-done((f32[160,640]{1,0:T(8,128)S(1)}, f32[160,640]{1,0:T(8,128)}, u32[]{:S(2)}, u32[]{:S(2)}) %collective-permute-start.4) | collective-permute-done | bytes 409632 | tf_op jit(solution)/shard_map/send1/ppermute | solution.py:314
  21.4 7.7 %sort.1.refs_0_ = f32[4,8,6400]{2,1,0:T(8,128)S(1)} custom-call(f32[2,4,25600]{2,1,0:T(4,128)S(1)} %copy-done), custom_call_target="tpu_custom_call" | custom-call | flops 8000000000 | bytes 24000000 | tf_op jit(solution)/shard_map/sort/pallas_call | solution.py:143
  29.1 0.2 join.1.refs_0_
  29.4 0.1 collective-permute-start.10
  29.4 2.8 %collective-permute-start.8 = (f32[160,640]{1,0:T(8,128)}, f32[160,640]{1,0:T(8,128)S(1)}, u32[]{:S(2)}, u32[]{:S(2)}) collective-permute-start(f32[160,640]{1,0:T(8,128)} %collective-permute-done.3.refs_3_), channel_id=1, source_target_pairs={{0,8},{1,9},{2,10},{3,11},{4,12},{5,13},{6,14},{7,15},{8,16},{9,17... | collective-permute-start | bytes 1228808 | tf_op jit(solution)/shard_map/send5/ppermute | solution.py:314
  32.2 1.3 collective-permute-start.9
  33.5 0.6 collective-permute-start.7
  34.1 7.7 %collective-permute-done.8.refs_6_ = f32[160,640]{1,0:T(8,128)S(1)} collective-permute-done((f32[160,640]{1,0:T(8,128)}, f32[160,640]{1,0:T(8,128)S(1)}, u32[]{:S(2)}, u32[]{:S(2)}) %collective-permute-start.8) | collective-permute-done | bytes 409632 | tf_op jit(solution)/shard_map/send5/ppermute | solution.py:314
  41.8 4.0 %collective-permute-done.9.refs_5_ = f32[160,640]{1,0:T(8,128)S(1)} collective-permute-done((f32[160,640]{1,0:T(8,128)}, f32[160,640]{1,0:T(8,128)S(1)}, u32[]{:S(2)}, u32[]{:S(2)}) %collective-permute-start.9) | collective-permute-done | bytes 409632 | tf_op jit(solution)/shard_map/send6/ppermute | solution.py:314
  45.9 3.5 %collective-permute-start.5 = (f32[160,640]{1,0:T(8,128)}, f32[160,640]{1,0:T(8,128)S(1)}, u32[]{:S(2)}, u32[]{:S(2)}) collective-permute-start(f32[160,640]{1,0:T(8,128)} %collective-permute-done.refs_3_), channel_id=1, source_target_pairs={{0,8},{1,9},{2,10},{3,11},{4,12},{5,13},{6,14},{7,15},{8,16},{9,17... | collective-permute-start | bytes 1228808 | tf_op jit(solution)/shard_map/send7/ppermute | solution.py:314
  49.4 1.3 collective-permute-start.6
  50.7 8.4 %collective-permute-done.5.refs_6_ = f32[160,640]{1,0:T(8,128)S(1)} collective-permute-done((f32[160,640]{1,0:T(8,128)}, f32[160,640]{1,0:T(8,128)S(1)}, u32[]{:S(2)}, u32[]{:S(2)}) %collective-permute-start.5) | collective-permute-done | bytes 409632 | tf_op jit(solution)/shard_map/send7/ppermute | solution.py:314
  59.0 4.0 %collective-permute-done.6.refs_5_ = f32[160,640]{1,0:T(8,128)S(1)} collective-permute-done((f32[160,640]{1,0:T(8,128)}, f32[160,640]{1,0:T(8,128)S(1)}, u32[]{:S(2)}, u32[]{:S(2)}) %collective-permute-start.6) | collective-permute-done | bytes 409632 | tf_op jit(solution)/shard_map/send8/ppermute | solution.py:314
  63.1 2.9 %collective-permute-start.14 = (f32[160,640]{1,0:T(8,128)S(1)}, f32[160,640]{1,0:T(8,128)S(1)}, u32[]{:S(2)}, u32[]{:S(2)}) collective-permute-start(f32[160,640]{1,0:T(8,128)S(1)} %collective-permute-done.8.refs_6_), channel_id=1, source_target_pairs={{0,8},{1,9},{2,10},{3,11},{4,12},{5,13},{6,14},{7,15},{8,16},{9,17... | collective-permute-start | bytes 1228808 | tf_op jit(solution)/shard_map/send11/ppermute | solution.py:314
  66.0 1.3 collective-permute-start.15
  67.3 0.6 collective-permute-start.17
  67.9 4.6 %collective-permute-start.12 = (f32[160,640]{1,0:T(8,128)S(1)}, f32[160,640]{1,0:T(8,128)S(1)}, u32[]{:S(2)}, u32[]{:S(2)}) collective-permute-start(f32[160,640]{1,0:T(8,128)S(1)} %collective-permute-done.5.refs_6_), channel_id=1, source_target_pairs={{0,8},{1,9},{2,10},{3,11},{4,12},{5,13},{6,14},{7,15},{8,16},{9,17... | collective-permute-start | bytes 1228808 | tf_op jit(solution)/shard_map/send14/ppermute | solution.py:314
  72.4 1.5 collective-permute-start.13
  73.9 0.5 arrange.1
  74.4 1.3 collective-permute-done.14.refs_8_
  75.7 4.5 %collective-permute-done.15.refs_7_ = f32[160,640]{1,0:T(8,128)S(1)} collective-permute-done((f32[160,640]{1,0:T(8,128)S(1)}, f32[160,640]{1,0:T(8,128)S(1)}, u32[]{:S(2)}, u32[]{:S(2)}) %collective-permute-start.15) | collective-permute-done | bytes 409632 | tf_op jit(solution)/shard_map/send12/ppermute | solution.py:314
  80.2 5.6 %cycle.3 = (f32[160,640]{1,0:T(8,128)S(1)}, f32[160,640]{1,0:T(8,128)}) custom-call(bf16[4,320,640]{2,1,0:T(8,128)(2,1)S(1)} %get-tuple-element.110.refs_0_, bf16[4,320,640]{2,1,0:T(8,128)(2,1)S(1)} %get-tuple-element.111.refs_1_, f32[160,640]{1,0:T(8,128)S(1)} %get-tuple-element.106.refs_2_, f32[160,640]{1,0:T(8,128)} %collective-permute-done.3.refs_3_, ...), custom_call_target="tpu_custom_call" | custom-call | flops 7000000000 | bytes 21000000 | tf_op jit(solution)/shard_map/cycle/pallas_call | solution.py:143
  85.8 4.3 %cycle.4.refs_2_ = f32[320,640]{1,0:T(8,128)S(1)} custom-call(bf16[4,320,640]{2,1,0:T(8,128)(2,1)S(1)} %get-tuple-element.110.refs_0_, bf16[4,320,640]{2,1,0:T(8,128)(2,1)S(1)} %get-tuple-element.111.refs_1_, f32[160,640]{1,0:T(8,128)S(1)} %get-tuple-element.112.refs_2_, f32[160,640]{1,0:T(8,128)} %collective-permute-done.refs_3_, ...), custom_call_target="tpu_custom_call" | custom-call | flops 5800000000 | bytes 17400000 | tf_op jit(solution)/shard_map/cycle/pallas_call | solution.py:143
  90.1 0.9 copy-done.13
  91.0 0.8 copy-done.1
  91.8 0.8 copy-done.3
  92.5 1.5 collective-permute-start.19
  94.1 0.1 copy.9.info.window
  94.2 1.0 copy-done.2
  95.2 1.0 copy-done.4
  96.2 1.4 copy-done.10
  97.6 1.4 copy-done.12
  99.0 1.1 copy-done.14
  100.2 1.0 cycle.5
  101.1 3.6 %collective-permute-done.19.got_ref = f32[160,640]{1,0:T(8,128)} collective-permute-done((f32[160,640]{1,0:T(8,128)}, f32[160,640]{1,0:T(8,128)}, u32[]{:S(2)}, u32[]{:S(2)}) %collective-permute-start.19) | collective-permute-done | bytes 409632 | tf_op jit(solution)/shard_map/send18/ppermute | solution.py:314
  104.7 1.3 add.8
  106.0 1.6 collective-permute-start.20
  107.6 1.9 %collective-permute-start.21 = (f32[160,320]{1,0:T(8,128)S(1)}, f32[160,320]{1,0:T(8,128)S(1)}, u32[]{:S(2)}, u32[]{:S(2)}) collective-permute-start(f32[160,320]{1,0:T(8,128)S(1)} %get-tuple-element.141), channel_id=1, source_target_pairs={{0,0},{1,8},{2,16},{3,24},{4,4},{5,12},{6,20},{7,28},{8,1},{9,9},{... | collective-permute-start | bytes 614408 | tf_op jit(solution)/shard_map/send21/ppermute | solution.py:314
  109.5 3.8 %collective-permute-start.22 = (f32[160,320]{1,0:T(8,128)S(1)}, f32[160,320]{1,0:T(8,128)S(1)}, u32[]{:S(2)}, u32[]{:S(2)}) collective-permute-start(f32[160,320]{1,0:T(8,128)S(1)} %get-tuple-element.142), channel_id=1, source_target_pairs={{0,4},{1,12},{2,20},{3,28},{4,0},{5,8},{6,16},{7,24},{8,5},{9,13},... | collective-permute-start | bytes 614408 | tf_op jit(solution)/shard_map/send22/ppermute | solution.py:314
  113.3 10.8 %ladder.2 = f32[2,2,32,200]{3,2,1,0:T(8,128)S(1)} custom-call(s32[4,2]{1,0:T(4,128)S(1)} %copy.9.info.window, f32[4,8,6400]{2,1,0:T(8,128)S(1)} %sort.1.refs_0_, f32[4,8,6400]{2,1,0:T(8,128)S(1)} %collective-permute-done.11.refs_1_, f32[4,8,6400]{2,1,0:T(8,128)S(1)} %collective-permute-done.17.refs_2_, f32[4,8,6400]{2,1,0:T(8,128)S(1)} %collective-permute-done.18.refs_3_, ...), custom_call_target="tpu_custom_call" | custom-call | flops 11000000512 | bytes 33000000 | tf_op jit(solution)/shard_map/ladder/pallas_call | solution.py:118
  124.1 0.3 add.9
  124.5 10.8 %ladder.3 = f32[2,2,32,200]{3,2,1,0:T(8,128)S(1)} custom-call(s32[4,2]{1,0:T(4,128)S(1)} %copy.9.info.window, f32[4,8,6400]{2,1,0:T(8,128)S(1)} %sort.1.refs_0_, f32[4,8,6400]{2,1,0:T(8,128)S(1)} %collective-permute-done.11.refs_1_, f32[4,8,6400]{2,1,0:T(8,128)S(1)} %collective-permute-done.17.refs_2_, f32[4,8,6400]{2,1,0:T(8,128)S(1)} %collective-permute-done.18.refs_3_, ...), custom_call_target="tpu_custom_call" | custom-call | flops 11000000512 | bytes 33000000 | tf_op jit(solution)/shard_map/ladder/pallas_call | solution.py:118
  135.3 0.6 copy-done.5
  136.0 0.1 collective-permute-start.25
  136.2 1.8 %collective-permute-start.27 = (f32[4,2,8,200]{3,2,1,0:T(8,128)S(1)}, f32[4,2,8,200]{3,2,1,0:T(8,128)S(1)}, u32[]{:S(2)}, u32[]{:S(2)}) collective-permute-start(f32[4,2,8,200]{3,2,1,0:T(8,128)S(1)} %get-tuple-element.158), channel_id=1, source_target_pairs={{0,3},{1,2},{2,1},{3,0},{4,7},{5,6},{6,5},{7,4},{8,11},{9,10},{10,... | collective-permute-start | bytes 153608 | tf_op jit(solution)/shard_map/send27/ppermute | solution.py:314
  138.0 2.2 %collective-permute-start.23 = (f32[160,320]{1,0:T(8,128)}, f32[160,320]{1,0:T(8,128)S(1)}, u32[]{:S(2)}, u32[]{:S(2)}) collective-permute-start(f32[160,320]{1,0:T(8,128)} %copy-done.8), channel_id=1, source_target_pairs={{0,0},{1,8},{2,16},{3,24},{4,4},{5,12},{6,20},{7,28},{8,1},{9,9},{... | collective-permute-start | bytes 614408 | tf_op jit(solution)/shard_map/send23/ppermute | solution.py:314
  140.2 4.8 %collective-permute-start.24 = (f32[160,320]{1,0:T(8,128)}, f32[160,320]{1,0:T(8,128)S(1)}, u32[]{:S(2)}, u32[]{:S(2)}) collective-permute-start(f32[160,320]{1,0:T(8,128)} %copy-done.7), channel_id=1, source_target_pairs={{0,4},{1,12},{2,20},{3,28},{4,0},{5,8},{6,16},{7,24},{8,5},{9,13},... | collective-permute-start | bytes 614408 | tf_op jit(solution)/shard_map/send24/ppermute | solution.py:314
  145.1 0.1 copy.7
  145.2 0.3 slice.37.early_ref
  145.5 0.3 slice.39.late_ref
  145.8 13.6 %collective-permute-done.23.s1_ref = f32[160,320]{1,0:T(8,128)S(1)} collective-permute-done((f32[160,320]{1,0:T(8,128)}, f32[160,320]{1,0:T(8,128)S(1)}, u32[]{:S(2)}, u32[]{:S(2)}) %collective-permute-start.23) | collective-permute-done | bytes 204832 | tf_op jit(solution)/shard_map/send23/ppermute | solution.py:314
  159.4 5.2 %collective-permute-done.24.c1_ref = f32[160,320]{1,0:T(8,128)S(1)} collective-permute-done((f32[160,320]{1,0:T(8,128)}, f32[160,320]{1,0:T(8,128)S(1)}, u32[]{:S(2)}, u32[]{:S(2)}) %collective-permute-start.24) | collective-permute-done | bytes 204832 | tf_op jit(solution)/shard_map/send24/ppermute | solution.py:314
  164.6 1.0 copy-done.18
  165.6 2.1 %merge.1 = f32[2,4,160,160]{3,2,1,0:T(8,128)S(1)} custom-call(s32[4,2]{1,0:T(4,128)S(1)} %copy.9.info.window, f32[160,640]{1,0:T(8,128)S(1)} %copy-done.16, f32[160,640]{1,0:T(8,128)S(1)} %copy-done.18, f32[160,320]{1,0:T(8,128)S(1)} %collective-permute-done.21.s0_ref, f32[160,320]{1,0:T(8,128)S(1)} %copy-done.6, ...), custom_call_target="tpu_custom_call" | custom-call | flops 2000000000 | bytes 6000000 | tf_op jit(solution)/shard_map/merge/pallas_call | solution.py:143
  167.7 1.9 %reshape.14 = f32[2,4,25600]{2,1,0:T(4,128)} reshape(f32[2,4,160,160]{3,2,1,0:T(8,128)S(1)} %merge.1) | data formatting | bytes 1638400 | tf_op jit(solution)/shard_map/reshape | solution.py:409
  (64 shorter events, 0.4 us)
Async XLA Ops:
  2.0 12.9 %copy-start = (f32[2,4,25600]{2,1,0:T(4,128)S(1)}, f32[2,4,25600]{2,1,0:T(4,128)}, u32[]{:S(2)}) copy-start(f32[2,4,25600]{2,1,0:T(4,128)} %flat_ref) | copy-start | bytes 2457604
  2.8 15.3 %collective-permute-start.3 = (f32[160,640]{1,0:T(8,128)S(1)}, f32[160,640]{1,0:T(8,128)}, u32[]{:S(2)}, u32[]{:S(2)}) collective-permute-start(f32[160,640]{1,0:T(8,128)S(1)} %get-tuple-element.106.refs_2_), channel_id=1, source_target_pairs={{0,8},{1,9},{2,10},{3,11},{4,12},{5,13},{6,14},{7,15},{8,16},{9,17... | collective-permute-start | bytes 1228808 | tf_op jit(solution)/shard_map/send0/ppermute | solution.py:314
  7.0 14.4 %collective-permute-start.4 = (f32[160,640]{1,0:T(8,128)S(1)}, f32[160,640]{1,0:T(8,128)}, u32[]{:S(2)}, u32[]{:S(2)}) collective-permute-start(f32[160,640]{1,0:T(8,128)S(1)} %get-tuple-element.106.refs_2_), channel_id=1, source_target_pairs={{8,0},{9,1},{10,2},{11,3},{12,4},{13,5},{14,6},{15,7},{16,8},{17,9... | collective-permute-start | bytes 1228808 | tf_op jit(solution)/shard_map/send1/ppermute | solution.py:314
  8.3 20.8 %collective-permute-start = (f32[160,640]{1,0:T(8,128)S(1)}, f32[160,640]{1,0:T(8,128)}, u32[]{:S(2)}, u32[]{:S(2)}) collective-permute-start(f32[160,640]{1,0:T(8,128)S(1)} %get-tuple-element.112.refs_2_), channel_id=1, source_target_pairs={{0,8},{1,9},{2,10},{3,11},{4,12},{5,13},{6,14},{7,15},{8,16},{9,17... | collective-permute-start | bytes 1228808 | tf_op jit(solution)/shard_map/send2/ppermute | solution.py:314
  13.6 15.5 %collective-permute-start.1 = (f32[160,640]{1,0:T(8,128)S(1)}, f32[160,640]{1,0:T(8,128)}, u32[]{:S(2)}, u32[]{:S(2)}) collective-permute-start(f32[160,640]{1,0:T(8,128)S(1)} %get-tuple-element.112.refs_2_), channel_id=1, source_target_pairs={{8,0},{9,1},{10,2},{11,3},{12,4},{13,5},{14,6},{15,7},{16,8},{17,9... | collective-permute-start | bytes 1228808 | tf_op jit(solution)/shard_map/send3/ppermute | solution.py:314
  16.5 12.6 %collective-permute-start.2 = (f32[160,640]{1,0:T(8,128)S(1)}, f32[160,640]{1,0:T(8,128)S(1)}, u32[]{:S(2)}, u32[]{:S(2)}) collective-permute-start(f32[160,640]{1,0:T(8,128)S(1)} %get-tuple-element.82), channel_id=1, source_target_pairs={{0,4},{1,5},{2,6},{3,7},{4,0},{5,1},{6,2},{7,3},{8,12},{9,13},{10,... | collective-permute-start | bytes 1228808 | tf_op jit(solution)/shard_map/send4/ppermute | solution.py:314
  29.4 16.5 %collective-permute-start.10 = (f32[320,640]{1,0:T(8,128)S(1)}, f32[320,640]{1,0:T(8,128)S(1)}, u32[]{:S(2)}, u32[]{:S(2)}) collective-permute-start(f32[320,640]{1,0:T(8,128)S(1)} %join.1.refs_0_), channel_id=1, source_target_pairs={{0,1},{1,0},{2,3},{3,2},{4,5},{5,4},{6,7},{7,6},{8,9},{9,8},{10,11... | collective-permute-start | bytes 2457608 | tf_op jit(solution)/shard_map/send10/ppermute | solution.py:314
  29.4 12.4 %collective-permute-start.8 = (f32[160,640]{1,0:T(8,128)}, f32[160,640]{1,0:T(8,128)S(1)}, u32[]{:S(2)}, u32[]{:S(2)}) collective-permute-start(f32[160,640]{1,0:T(8,128)} %collective-permute-done.3.refs_3_), channel_id=1, source_target_pairs={{0,8},{1,9},{2,10},{3,11},{4,12},{5,13},{6,14},{7,15},{8,16},{9,17... | collective-permute-start | bytes 1228808 | tf_op jit(solution)/shard_map/send5/ppermute | solution.py:314
  32.2 13.7 %collective-permute-start.9 = (f32[160,640]{1,0:T(8,128)}, f32[160,640]{1,0:T(8,128)S(1)}, u32[]{:S(2)}, u32[]{:S(2)}) collective-permute-start(f32[160,640]{1,0:T(8,128)} %collective-permute-done.4.refs_4_), channel_id=1, source_target_pairs={{8,0},{9,1},{10,2},{11,3},{12,4},{13,5},{14,6},{15,7},{16,8},{17,9... | collective-permute-start | bytes 1228808 | tf_op jit(solution)/shard_map/send6/ppermute | solution.py:314
  33.5 29.6 %collective-permute-start.7 = (f32[320,640]{1,0:T(8,128)S(1)}, f32[320,640]{1,0:T(8,128)S(1)}, u32[]{:S(2)}, u32[]{:S(2)}) collective-permute-start(f32[320,640]{1,0:T(8,128)S(1)} %join.1.refs_0_), channel_id=1, source_target_pairs={{0,2},{1,3},{2,0},{3,1},{4,6},{5,7},{6,4},{7,5},{8,10},{9,11},{10,... | collective-permute-start | bytes 2457608 | tf_op jit(solution)/shard_map/send9/ppermute | solution.py:314
  45.9 17.2 %collective-permute-start.11 = (f32[4,8,6400]{2,1,0:T(8,128)S(1)}, f32[4,8,6400]{2,1,0:T(8,128)S(1)}, u32[]{:S(2)}, u32[]{:S(2)}) collective-permute-start(f32[4,8,6400]{2,1,0:T(8,128)S(1)} %sort.1.refs_0_), channel_id=1, source_target_pairs={{0,1},{1,0},{2,3},{3,2},{4,5},{5,4},{6,7},{7,6},{8,9},{9,8},{10,11... | collective-permute-start | bytes 2457608 | tf_op jit(solution)/shard_map/send13/ppermute | solution.py:314
  45.9 13.2 %collective-permute-start.5 = (f32[160,640]{1,0:T(8,128)}, f32[160,640]{1,0:T(8,128)S(1)}, u32[]{:S(2)}, u32[]{:S(2)}) collective-permute-start(f32[160,640]{1,0:T(8,128)} %collective-permute-done.refs_3_), channel_id=1, source_target_pairs={{0,8},{1,9},{2,10},{3,11},{4,12},{5,13},{6,14},{7,15},{8,16},{9,17... | collective-permute-start | bytes 1228808 | tf_op jit(solution)/shard_map/send7/ppermute | solution.py:314
  49.4 13.7 %collective-permute-start.6 = (f32[160,640]{1,0:T(8,128)}, f32[160,640]{1,0:T(8,128)S(1)}, u32[]{:S(2)}, u32[]{:S(2)}) collective-permute-start(f32[160,640]{1,0:T(8,128)} %collective-permute-done.1.refs_4_), channel_id=1, source_target_pairs={{8,0},{9,1},{10,2},{11,3},{12,4},{13,5},{14,6},{15,7},{16,8},{17,9... | collective-permute-start | bytes 1228808 | tf_op jit(solution)/shard_map/send8/ppermute | solution.py:314
  63.1 9.4 %collective-permute-start.16 = (f32[320,640]{1,0:T(8,128)S(1)}, f32[320,640]{1,0:T(8,128)S(1)}, u32[]{:S(2)}, u32[]{:S(2)}) collective-permute-start(f32[320,640]{1,0:T(8,128)S(1)} %collective-permute-done.7.refs_2_), channel_id=1, source_target_pairs={{0,1},{1,0},{2,3},{3,2},{4,5},{5,4},{6,7},{7,6},{8,9},{9,8},{10,11... | collective-permute-start | bytes 2457608 | tf_op jit(solution)/shard_map/send16/ppermute | solution.py:314
  63.1 12.6 %collective-permute-start.14 = (f32[160,640]{1,0:T(8,128)S(1)}, f32[160,640]{1,0:T(8,128)S(1)}, u32[]{:S(2)}, u32[]{:S(2)}) collective-permute-start(f32[160,640]{1,0:T(8,128)S(1)} %collective-permute-done.8.refs_6_), channel_id=1, source_target_pairs={{0,8},{1,9},{2,10},{3,11},{4,12},{5,13},{6,14},{7,15},{8,16},{9,17... | collective-permute-start | bytes 1228808 | tf_op jit(solution)/shard_map/send11/ppermute | solution.py:314
  66.0 14.2 %collective-permute-start.15 = (f32[160,640]{1,0:T(8,128)S(1)}, f32[160,640]{1,0:T(8,128)S(1)}, u32[]{:S(2)}, u32[]{:S(2)}) collective-permute-start(f32[160,640]{1,0:T(8,128)S(1)} %collective-permute-done.9.refs_5_), channel_id=1, source_target_pairs={{8,0},{9,1},{10,2},{11,3},{12,4},{13,5},{14,6},{15,7},{16,8},{17,9... | collective-permute-start | bytes 1228808 | tf_op jit(solution)/shard_map/send12/ppermute | solution.py:314
  67.3 25.3 %collective-permute-start.17 = (f32[4,8,6400]{2,1,0:T(8,128)S(1)}, f32[4,8,6400]{2,1,0:T(8,128)S(1)}, u32[]{:S(2)}, u32[]{:S(2)}) collective-permute-start(f32[4,8,6400]{2,1,0:T(8,128)S(1)} %sort.1.refs_0_), channel_id=1, source_target_pairs={{0,2},{1,3},{2,0},{3,1},{4,6},{5,7},{6,4},{7,5},{8,10},{9,11},{10,... | collective-permute-start | bytes 2457608 | tf_op jit(solution)/shard_map/send17/ppermute | solution.py:314
  67.9 23.1 %collective-permute-start.12 = (f32[160,640]{1,0:T(8,128)S(1)}, f32[160,640]{1,0:T(8,128)S(1)}, u32[]{:S(2)}, u32[]{:S(2)}) collective-permute-start(f32[160,640]{1,0:T(8,128)S(1)} %collective-permute-done.5.refs_6_), channel_id=1, source_target_pairs={{0,8},{1,9},{2,10},{3,11},{4,12},{5,13},{6,14},{7,15},{8,16},{9,17... | collective-permute-start | bytes 1228808 | tf_op jit(solution)/shard_map/send14/ppermute | solution.py:314
  72.4 19.3 %collective-permute-start.13 = (f32[160,640]{1,0:T(8,128)S(1)}, f32[160,640]{1,0:T(8,128)S(1)}, u32[]{:S(2)}, u32[]{:S(2)}) collective-permute-start(f32[160,640]{1,0:T(8,128)S(1)} %collective-permute-done.6.refs_5_), channel_id=1, source_target_pairs={{8,0},{9,1},{10,2},{11,3},{12,4},{13,5},{14,6},{15,7},{16,8},{17,9... | collective-permute-start | bytes 1228808 | tf_op jit(solution)/shard_map/send15/ppermute | solution.py:314
  74.4 11.4 %copy-start.9 = (bf16[4,320,640]{2,1,0:T(8,128)(2,1)}, bf16[4,320,640]{2,1,0:T(8,128)(2,1)S(1)}, u32[]{:S(2)}) copy-start(bf16[4,320,640]{2,1,0:T(8,128)(2,1)S(1)} %get-tuple-element.110.refs_0_) | copy-start | bytes 4915204
  74.4 11.4 %copy-start.11 = (bf16[4,320,640]{2,1,0:T(8,128)(2,1)}, bf16[4,320,640]{2,1,0:T(8,128)(2,1)S(1)}, u32[]{:S(2)}) copy-start(bf16[4,320,640]{2,1,0:T(8,128)(2,1)S(1)} %get-tuple-element.111.refs_1_) | copy-start | bytes 4915204
  85.8 4.3 %copy-start.19 = (f32[160,640]{1,0:T(8,128)}, f32[160,640]{1,0:T(8,128)S(1)}, u32[]{:S(2)}) copy-start(f32[160,640]{1,0:T(8,128)S(1)} %get-tuple-element.120.keep_ref) | copy-start | bytes 1228804
  85.8 8.3 %copy-start.21 = (s32[4,2]{0,1:T(2,128)S(1)}, s32[4,2]{0,1:T(2,128)}, u32[]{:S(2)}) copy-start(s32[4,2]{0,1:T(2,128)} %param.7) | copy-start | bytes 100
  90.1 0.9 copy-start.13
  91.0 0.8 copy-start.1
  91.7 0.8 copy-start.3
  92.5 12.2 %collective-permute-start.18 = (f32[4,8,6400]{2,1,0:T(8,128)S(1)}, f32[4,8,6400]{2,1,0:T(8,128)S(1)}, u32[]{:S(2)}, u32[]{:S(2)}) collective-permute-start(f32[4,8,6400]{2,1,0:T(8,128)S(1)} %collective-permute-done.17.refs_2_), channel_id=1, source_target_pairs={{0,1},{1,0},{2,3},{3,2},{4,5},{5,4},{6,7},{7,6},{8,9},{9,8},{10,11... | collective-permute-start | bytes 2457608 | tf_op jit(solution)/shard_map/send19/ppermute | solution.py:314
  92.5 12.2 %collective-permute-start.19 = (f32[160,640]{1,0:T(8,128)}, f32[160,640]{1,0:T(8,128)}, u32[]{:S(2)}, u32[]{:S(2)}) collective-permute-start(f32[160,640]{1,0:T(8,128)} %get-tuple-element.118), channel_id=1, source_target_pairs={{0,4},{1,5},{2,6},{3,7},{4,0},{5,1},{6,2},{7,3},{8,12},{9,13},{10,... | collective-permute-start | bytes 1228808 | tf_op jit(solution)/shard_map/send18/ppermute | solution.py:314
  94.2 1.0 copy-start.2
  95.2 1.0 copy-start.4
  96.2 1.4 copy-start.10
  97.6 1.4 copy-start.12
  99.0 1.1 copy-start.14
  100.2 4.6 %copy-start.20 = (f32[160,640]{1,0:T(8,128)S(1)}, f32[160,640]{1,0:T(8,128)}, u32[]{:S(2)}) copy-start(f32[160,640]{1,0:T(8,128)} %copy-done.19) | copy-start | bytes 1228804
  106.0 18.1 %copy-start.15 = (f32[160,640]{1,0:T(8,128)}, f32[160,640]{1,0:T(8,128)S(1)}, u32[]{:S(2)}) copy-start(f32[160,640]{1,0:T(8,128)S(1)} %get-tuple-element.125.zero_ref) | copy-start | bytes 1228804
  106.0 18.1 %collective-permute-start.20 = (f32[160,640]{1,0:T(8,128)S(1)}, f32[160,640]{1,0:T(8,128)S(1)}, u32[]{:S(2)}, u32[]{:S(2)}) collective-permute-start(f32[160,640]{1,0:T(8,128)S(1)} %get-tuple-element.127), channel_id=1, source_target_pairs={{0,4},{1,5},{2,6},{3,7},{4,0},{5,1},{6,2},{7,3},{8,12},{9,13},{10,... | collective-permute-start | bytes 1228808 | tf_op jit(solution)/shard_map/send20/ppermute | solution.py:314
  107.6 27.7 %collective-permute-start.21 = (f32[160,320]{1,0:T(8,128)S(1)}, f32[160,320]{1,0:T(8,128)S(1)}, u32[]{:S(2)}, u32[]{:S(2)}) collective-permute-start(f32[160,320]{1,0:T(8,128)S(1)} %get-tuple-element.141), channel_id=1, source_target_pairs={{0,0},{1,8},{2,16},{3,24},{4,4},{5,12},{6,20},{7,28},{8,1},{9,9},{... | collective-permute-start | bytes 614408 | tf_op jit(solution)/shard_map/send21/ppermute | solution.py:314
  109.5 25.8 %collective-permute-start.22 = (f32[160,320]{1,0:T(8,128)S(1)}, f32[160,320]{1,0:T(8,128)S(1)}, u32[]{:S(2)}, u32[]{:S(2)}) collective-permute-start(f32[160,320]{1,0:T(8,128)S(1)} %get-tuple-element.142), channel_id=1, source_target_pairs={{0,4},{1,12},{2,20},{3,28},{4,0},{5,8},{6,16},{7,24},{8,5},{9,13},... | collective-permute-start | bytes 614408 | tf_op jit(solution)/shard_map/send22/ppermute | solution.py:314
  124.4 10.8 %copy-start.7 = (f32[160,320]{1,0:T(8,128)}, f32[160,320]{1,0:T(8,128)S(1)}, u32[]{:S(2)}) copy-start(f32[160,320]{1,0:T(8,128)S(1)} %get-tuple-element.150) | copy-start | bytes 614404
  124.4 10.8 %copy-start.8 = (f32[160,320]{1,0:T(8,128)}, f32[160,320]{1,0:T(8,128)S(1)}, u32[]{:S(2)}) copy-start(f32[160,320]{1,0:T(8,128)S(1)} %get-tuple-element.149) | copy-start | bytes 614404
  124.4 10.8 %copy-start.17 = (f32[160,640]{1,0:T(8,128)}, f32[160,640]{1,0:T(8,128)S(1)}, u32[]{:S(2)}) copy-start(f32[160,640]{1,0:T(8,128)S(1)} %get-tuple-element.140.one_ref) | copy-start | bytes 1228804
  135.3 0.7 copy-start.5
  136.0 8.9 %collective-permute-start.25 = (f32[4,2,8,200]{3,2,1,0:T(8,128)S(1)}, f32[4,2,8,200]{3,2,1,0:T(8,128)S(1)}, u32[]{:S(2)}, u32[]{:S(2)}) collective-permute-start(f32[4,2,8,200]{3,2,1,0:T(8,128)S(1)} %get-tuple-element.160), channel_id=1, source_target_pairs={{0,1},{1,0},{2,3},{3,2},{4,5},{5,4},{6,7},{7,6},{8,9},{9,8},{10,11... | collective-permute-start | bytes 153608 | tf_op jit(solution)/shard_map/send25/ppermute | solution.py:314
  136.1 8.8 %collective-permute-start.26 = (f32[4,2,8,200]{3,2,1,0:T(8,128)S(1)}, f32[4,2,8,200]{3,2,1,0:T(8,128)S(1)}, u32[]{:S(2)}, u32[]{:S(2)}) collective-permute-start(f32[4,2,8,200]{3,2,1,0:T(8,128)S(1)} %get-tuple-element.159), channel_id=1, source_target_pairs={{0,2},{1,3},{2,0},{3,1},{4,6},{5,7},{6,4},{7,5},{8,10},{9,11},{10,... | collective-permute-start | bytes 153608 | tf_op jit(solution)/shard_map/send26/ppermute | solution.py:314
  136.2 8.8 %collective-permute-start.27 = (f32[4,2,8,200]{3,2,1,0:T(8,128)S(1)}, f32[4,2,8,200]{3,2,1,0:T(8,128)S(1)}, u32[]{:S(2)}, u32[]{:S(2)}) collective-permute-start(f32[4,2,8,200]{3,2,1,0:T(8,128)S(1)} %get-tuple-element.158), channel_id=1, source_target_pairs={{0,3},{1,2},{2,1},{3,0},{4,7},{5,6},{6,5},{7,4},{8,11},{9,10},{10,... | collective-permute-start | bytes 153608 | tf_op jit(solution)/shard_map/send27/ppermute | solution.py:314
  138.0 21.4 %collective-permute-start.23 = (f32[160,320]{1,0:T(8,128)}, f32[160,320]{1,0:T(8,128)S(1)}, u32[]{:S(2)}, u32[]{:S(2)}) collective-permute-start(f32[160,320]{1,0:T(8,128)} %copy-done.8), channel_id=1, source_target_pairs={{0,0},{1,8},{2,16},{3,24},{4,4},{5,12},{6,20},{7,28},{8,1},{9,9},{... | collective-permute-start | bytes 614408 | tf_op jit(solution)/shard_map/send23/ppermute | solution.py:314
  140.2 24.4 %collective-permute-start.24 = (f32[160,320]{1,0:T(8,128)}, f32[160,320]{1,0:T(8,128)S(1)}, u32[]{:S(2)}, u32[]{:S(2)}) collective-permute-start(f32[160,320]{1,0:T(8,128)} %copy-done.7), channel_id=1, source_target_pairs={{0,4},{1,12},{2,20},{3,28},{4,0},{5,8},{6,16},{7,24},{8,5},{9,13},... | collective-permute-start | bytes 614408 | tf_op jit(solution)/shard_map/send24/ppermute | solution.py:314
  145.0 19.6 %copy-start.6 = (f32[160,320]{1,0:T(8,128)S(1)}, f32[160,320]{1,0:T(8,128)}, u32[]{:S(2)}) copy-start(f32[160,320]{1,0:T(8,128)} %copy-done.5) | copy-start | bytes 614404
  145.0 19.6 %copy-start.16 = (f32[160,640]{1,0:T(8,128)S(1)}, f32[160,640]{1,0:T(8,128)}, u32[]{:S(2)}) copy-start(f32[160,640]{1,0:T(8,128)} %copy-done.15) | copy-start | bytes 1228804
  164.6 1.0 copy-start.18
where the time goes:
time: 170 us
  waiting for transfers between devices  55.7 us (33%)
  starting transfers between devices  51.7 us (30%)
  Pallas kernels  46 us (27%)
  local copies, waits for them, and re-layouts  15.6 us (9%)
    ppermute x28, waiting for transfers between devices, send(): return lax.ppermute(a, AXES, permutation(rule))  55.7 us
    ppermute x28, starting transfers between devices, send(): return lax.ppermute(a, AXES, permutation(rule))  51.7 us
    pallas_call x11, Pallas kernels, whole(): pl.pallas_call(kernel, out_shape=[jax.ShapeDtypeStruct(shape, dtype) for...  24.4 us
    pallas_call x2, Pallas kernels, ladder_part(): pl.pallas_call(ladder_kernel, out_shape=jax.ShapeDtypeStruct((count, pair...  21.6 us
    unnamed x46, local copies, waits for them, and re-layouts  10.2 us
  transfers between devices with their start and end apart: 28, of which 10 were waited for; matrix products, arithmetic and copies ran while one was open for 1% of the time, Pallas kernels for 25%

commit v1 on v0

--- a/solution.py
+++ b/solution.py
@@ -168,10 +168,10 @@
             out_ref[kind, :, g * 4 * VI : (g + 1) * 4 * VI] = jnp.concatenate(line, axis=1)
 
 
-def turn_kernel(four_ref, zero_ref, one_ref):
+def turn_kernel(four_ref, out_ref):
     rows_i, cols_j, v, _ = four_ref.shape
-    for g, out_ref in enumerate((zero_ref, one_ref)):
-        out_ref[...] = jnp.concatenate(
+    for g in range(2):
+        out_ref[g * v : (g + 1) * v, :] = jnp.concatenate(
             [four_ref[k, 2 * h + g].T for h in range(2) for k in range(rows_i)], axis=1
         )
 
@@ -217,8 +217,6 @@
     z, y, _ = place()
     for plane in planes:
         x = refs.pop(0)[...]
-        if plane in ("two", "three"):
-            x = jnp.where(z < 2, x, refs.pop(0)[...])
         n = x.shape[1] // 2
         m = 2 * x.shape[0]
         high, low = split(jnp.concatenate([x[:, :n], x[:, n:]], axis=0))
@@ -236,22 +234,26 @@
     if not final:
         refs.pop(0)[...] = total
         return
-    keep_ref, give_ref = refs
-    v = total.shape[0] // 2
+    v = total.shape[0] // 4
     n = total.shape[1] // 2
-    sides = [
-        jnp.concatenate([total[h * v : (h + 1) * v, r * n : (r + 1) * n] for h in range(2)], axis=1)
-        for r in range(2)
-    ]
     low = y == 0
-    keep_ref[...] = jnp.where(low, sides[0], sides[1])
-    give_ref[...] = jnp.where(low, sides[1], sides[0])
+    for g in range(2):
+        sides = [
+            jnp.concatenate(
+                [total[(2 * h + g) * v : (2 * h + g + 1) * v, r * n : (r + 1) * n] for h in range(2)],
+                axis=1,
+            )
+            for r in range(2)
+        ]
+        keep_ref, give_ref = refs[2 * g : 2 * g + 2]
+        keep_ref[...] = jnp.where(low, sides[0], sides[1])
+        give_ref[...] = jnp.where(low, sides[1], sides[0])
 
 
 def cycle_part(high, low, chunks, acc, final):
     args = [high, low] + ([] if acc is None else [acc]) + [x for c in chunks for x in c[1]]
     v, n = chunks[0][1][0].shape
-    shapes = [(v, n)] * 2 if final else [(2 * v, n)]
+    shapes = [(v // 2, n)] * 4 if final else [(2 * v, n)]
     kernel = functools.partial(cycle_kernel, tuple(c[0] for c in chunks), acc is not None, final)
     return whole(kernel, "cycle", 1 + 1.2 * len(chunks), shapes, args)
 
@@ -259,31 +261,38 @@
 def add_kernel(keep_ref, got_ref, total_ref, same_ref, cross_ref):
     total = keep_ref[...] + got_ref[...]
     total_ref[...] = total
-    n = total.shape[1] // 2
+    v, n = total.shape[0] // 2, total.shape[1] // 2
+    sides = [
+        jnp.concatenate([total[:v, h * n : (h + 1) * n], total[v:, h * n : (h + 1) * n]], axis=1)
+        for h in range(2)
+    ]
     low = place()[1] == 0
-    same_ref[...] = jnp.where(low, total[:, :n], total[:, n:])
-    cross_ref[...] = jnp.where(low, total[:, n:], total[:, :n])
-
-
-def merge_kernel(window, zero_ref, one_ref, s0_ref, c0_ref, s1_ref, c1_ref, early_ref, late_ref, out_ref):
+    same_ref[...] = jnp.where(low, sides[0], sides[1])
+    cross_ref[...] = jnp.where(low, sides[1], sides[0])
+
+
+def merge_kernel(window, zero_ref, one_ref, s0_ref, c0_ref, s1_ref, c1_ref, ladder_ref, out_ref):
     rows_i, cols_j, v, _ = out_ref.shape
     low = place()[1] == 0
     totals = zero_ref, one_ref
     for i, (s_ref, c_ref) in enumerate(((s0_ref, c0_ref), (s1_ref, c1_ref))):
         same, cross = s_ref[...], c_ref[...]
-        image = jnp.where(low, same, cross), jnp.where(low, cross, same)
+        n = same.shape[1] // 2
+        image = [
+            jnp.concatenate([part[:, :n], part[:, n:]], axis=0)
+            for part in (jnp.where(low, same, cross), jnp.where(low, cross, same))
+        ]
         for j in range(cols_j):
             at = ((j // 2) * 2 + i) * v
             turned = totals[j % 2][:, at : at + v].T
             to = (j % 2) * v
             out_ref[i, j] = turned + image[j // 2][:, to : to + v]
     for which in range(NWIN):
-        source = (early_ref, late_ref)[which // 2]
         first, second = window[which, 0], window[which, 1]
         rows = pl.ds(pl.multiple_of(first * VI, 8), VI)
         for i in range(rows_i):
             for j in range(cols_j):
-                piece = source[which % 2, i, j]
+                piece = ladder_ref[which, i, j]
                 wide = jnp.concatenate(
                     [jnp.where(second == q, piece, 0.0) for q in range(NIRR)], axis=1
                 )
@@ -317,8 +326,9 @@
     swap_x = lambda a: send(a, lambda z, y, x, k: (z, y, 1 - x, k))
     swap_xk = lambda a: send(a, lambda z, y, x, k: (z, y, 1 - x, 1 - k))
     swap_y = lambda a: send(a, lambda z, y, x, k: (z, 1 - y, x, k))
-    up = lambda a: send(a, lambda z, y, x, k: (z + 1, y, x, k))
-    down = lambda a: send(a, lambda z, y, x, k: (z - 1, y, x, k))
+    up = lambda a, only: send(a, lambda z, y, x, k: (z + 1, y, x, k) if z in only else None)
+    down = lambda a, only: send(a, lambda z, y, x, k: (z - 1, y, x, k) if z in only else None)
+    ends = lambda a: send(a, lambda z, y, x, k: ({1: 0, 2: 3}[z], y, x, k) if z in (1, 2) else None)
     image = lambda a: send(a, lambda z, y, x, k: (2 * x + k, y, z // 2, z % 2))
     image_y = lambda a: send(a, lambda z, y, x, k: (2 * x + k, 1 - y, z // 2, z % 2))
     names = []
@@ -332,36 +342,33 @@
         count = laddered.shape[0]
         return jnp.transpose(got, (1, 3, 0, 2, 4)).reshape(count, rows_i, cols_j, VI, VI)
 
-    def products(own, a1, b1, a2, b2):
-        return [("own", [own]), ("below", [a1]), ("above", [b1]), ("two", [b2, a2])]
+    def products(own, a1, b1, c2):
+        return [("own", [own]), ("below", [a1]), ("above", [b1]), ("two", [c2])]
 
     def add(keep, got):
-        return whole(add_kernel, "add", 1, [slab] + [(v, slab[1] // 2)] * 2, (keep, got))
-
-    x0, x1 = whole(turn_kernel, "turn", 1.5, [slab] * 2, (cycle_int.reshape(four),))
-    a10, b10 = up(x0), down(x0)
-    a11, b11 = up(x1), down(x1)
-    amplitudes, x0, x1 = after((amplitudes, x0, x1))
+        return whole(add_kernel, "add", 1, [slab] + [(v // 2, slab[1])] * 2, (keep, got))
+
+    def ladder_of(begin, count):
+        return ladder_part(all_kinds, ladder_int, window, begin, count)
+
+    (x0,) = whole(turn_kernel, "turn", 1.5, [(rows_i * v, slab[1])], (cycle_int.reshape(four),))
+    a1, b1 = up(x0, (0, 1, 2)), down(x0, (1, 2, 3))
+    amplitudes, x0 = after((amplitudes, x0))
     keep, give = whole(pair_kernel, "pair", 1.5, [slab] * 2, (amplitudes.reshape(four),))
     got = swap_y(give)
-    a10, b10, keep, amplitudes = after((a10, b10, keep, amplitudes))
-
-    a20, b20 = up(a10), down(b10)
     (kinds,) = whole(
         sort_kernel, "sort", 8, [(NIRR, rows_i * cols_j, flat // NIRR)], (amplitudes,)
     )
-    a11, b11, got, kinds = after((a11, b11, got, kinds))
-
-    a21, b21 = up(a11), down(b11)
+    a1, b1, got, kinds = after((a1, b1, got, kinds))
+
+    a2, b2 = up(a1, (1, 2)), down(b1, (1, 2))
     (u,) = whole(join_kernel, "join", 1, [(rows_i * v, cols_j * v)], (keep, got))
     u_x, u_k = swap_x(u), swap(u)
-    a20, b20, u, u_k, kinds = after((a20, b20, u, u_k, kinds))
-
-    a30, b30 = up(a20), down(b20)
     kinds_k = swap(kinds)
-    a21, b21, u_x, kinds, kinds_k = after((a21, b21, u_x, kinds, kinds_k))
-
-    a31, b31 = up(a21), down(b21)
+    a2, b2, u_x, u_k, kinds, kinds_k = after((a2, b2, u_x, u_k, kinds, kinds_k))
+
+    c2 = jnp.where(lax.axis_index("row") < 4, b2, a2)
+    c3 = ends(c2)
     u_xk, kinds_x = swap(u_x), swap_x(kinds)
     high, low = whole(
         arrange_kernel,
@@ -372,38 +379,30 @@
         None,
         jnp.bfloat16,
     )
-    a30, b30, high, low = after((a30, b30, high, low))
-
-    keep0, give0 = cycle_part(
-        high, low, products(x0, a10, b10, a20, b20) + [("three", [b30, a30])], None, True
-    )
-    high, low, give0 = after((high, low, give0))
+    (part,) = cycle_part(high, low, products(x0, a1, b1, c2), None, False)
+    c3, part, kinds_x = after((c3, part, kinds_x))
+
+    keep0, give0, keep1, give1 = cycle_part(high, low, [("three", [c3])], part, True)
+    give0, give1, kinds_x = after((give0, give1, kinds_x))
     got0 = swap_y(give0)
-    (part,) = cycle_part(high, low, products(x1, a11, b11, a21, b21), None, False)
-    a31, b31, part, kinds_x = after((a31, b31, part, kinds_x))
-
-    keep1, give1 = cycle_part(high, low, [("three", [b31, a31])], part, True)
-    kinds_xk = swap(kinds_x)
-    give1, kinds_xk, got0 = after((give1, kinds_xk, got0))
+    all_kinds = (kinds, kinds_k, kinds_x, swap(kinds_x))
+    early = ladder_of(0, 2)
+    got0, early, all_kinds, give1 = after((got0, early, all_kinds, give1))
+
+    total0, same0, cross0 = add(keep0, got0)
     got1 = swap_y(give1)
-    total0, same0, cross0 = add(keep0, got0)
-    all_kinds, total0, same0, cross0 = after(((kinds, kinds_k, kinds_x, kinds_xk), total0, same0, cross0))
     same0, cross0 = image(same0), image_y(cross0)
-    early = ladder_part(all_kinds, ladder_int, window, 0, 2)
-    got1, early, all_kinds = after((got1, early, all_kinds))
-
+    late = ladder_of(2, 2)
+    got1, late = after((got1, late))
     total1, same1, cross1 = add(keep1, got1)
-    same1, cross1, total1, all_kinds = after((same1, cross1, total1, all_kinds))
     same1, cross1 = image(same1), image_y(cross1)
-    late = ladder_part(all_kinds, ladder_int, window, 2, 2)
-    same0, cross0, late = after((same0, cross0, late))
-    both = returned(jnp.concatenate([early, late]))
+    ladder = returned(jnp.concatenate([early, late]))
     (merged,) = whole(
         merge_kernel,
         "merge",
         2,
         [four],
-        (total0, total1, same0, cross0, same1, cross1, both[:2], both[2:]),
+        (total0, total1, same0, cross0, same1, cross1, ladder),
         window,
     )
     return merged.reshape(rows_i, cols_j, flat)

time: 170 us -> 148 us (0.87)
  starting transfers between devices: 51.7 us -> 30.8 us
  local copies, waits for them, and re-layouts: 15.6 us -> 10.5 us
  waiting for transfers between devices: 55.7 us -> 59.2 us
    ppermute x28 -> x21, starting transfers between devices: 51.7 us -> 30.8 us  [send(): return lax.ppermute(a, AXES, permutation(rule))]
    unnamed x46 -> x32, local copies, waits for them, and re-layouts: 10.2 us -> 5.2 us
    ppermute x28 -> x21, waiting for transfers between devices: 55.7 us -> 59.2 us  [send(): return lax.ppermute(a, AXES, permutation(rule))]
    pallas_call x11 -> x10, Pallas kernels: 24.4 us -> 23.8 us  [whole(): pl.pallas_call(kernel, out_shape=[jax.ShapeDtypeStruct(shape, dtype) for...]
  transfers between devices with their start and end apart: 28 -> 21, of which waited for: 10 -> 10; matrix products, arithmetic and copies ran while one was open for 1% -> 2% of each run, Pallas kernels for 25% -> 27%
where the time goes in v1:
time: 148 us
  waiting for transfers between devices  59.2 us (40%)
  Pallas kernels  45.4 us (31%)
  starting transfers between devices  30.8 us (21%)
  local copies, waits for them, and re-layouts  10.5 us (7%)
    ppermute x21, waiting for transfers between devices, send(): return lax.ppermute(a, AXES, permutation(rule))  59.2 us
    ppermute x21, starting transfers between devices, send(): return lax.ppermute(a, AXES, permutation(rule))  30.8 us
    pallas_call x10, Pallas kernels, whole(): pl.pallas_call(kernel, out_shape=[jax.ShapeDtypeStruct(shape, dtype) for...  23.8 us
    pallas_call x2, Pallas kernels, ladder_part(): pl.pallas_call(ladder_kernel, out_shape=jax.ShapeDtypeStruct((count, pair...  21.6 us
    unnamed x32, local copies, waits for them, and re-layouts  5.2 us
  transfers between devices with their start and end apart: 21, of which 10 were waited for; matrix products, arithmetic and copies ran while one was open for 2% of the time, Pallas kernels for 27%

profile of v1, /device:TPU:2, one launch (start us, length us, event | category | flops | bytes accessed | tf_op | source)
XLA Modules:
  0.0 147.6 jit_solution(5717912062571645745)
XLA Ops:
  0.0 2.0 %reshape.12.four_ref = f32[2,4,160,160]{3,2,1,0:T(8,128)S(1)} reshape(f32[2,4,25600]{2,1,0:T(4,128)} %param.5) | data formatting | bytes 1638400 | tf_op jit(solution)/shard_map/reshape | solution.py:354
  2.0 0.0 copy-start
  2.0 0.8 turn.1.refs_2_
  2.8 4.4 %collective-permute-start = (f32[320,640]{1,0:T(8,128)S(1)}, f32[320,640]{1,0:T(8,128)}, u32[]{:S(2)}, u32[]{:S(2)}) collective-permute-start(f32[320,640]{1,0:T(8,128)S(1)} %turn.1.refs_2_), channel_id=1, source_target_pairs={{0,8},{1,9},{2,10},{3,11},{4,12},{5,13},{6,14},{7,15},{8,16},{9,17... | collective-permute-start | bytes 2457608 | tf_op jit(solution)/shard_map/send0/ppermute | solution.py:323
  7.2 1.3 collective-permute-start.1
  8.5 0.8 reshape.13.four_ref
  9.3 0.8 pair.1
  10.1 1.6 %collective-permute-start.2 = (f32[160,640]{1,0:T(8,128)S(1)}, f32[160,640]{1,0:T(8,128)S(1)}, u32[]{:S(2)}, u32[]{:S(2)}) collective-permute-start(f32[160,640]{1,0:T(8,128)S(1)} %get-tuple-element.48), channel_id=1, source_target_pairs={{0,4},{1,5},{2,6},{3,7},{4,0},{5,1},{6,2},{7,3},{8,12},{9,13},{10,... | collective-permute-start | bytes 1228808 | tf_op jit(solution)/shard_map/send2/ppermute | solution.py:323
  11.7 7.7 %sort.1.refs_0_ = f32[4,8,6400]{2,1,0:T(8,128)S(1)} custom-call(f32[2,4,25600]{2,1,0:T(4,128)S(1)} %copy-done), custom_call_target="tpu_custom_call" | custom-call | flops 8000000000 | bytes 24000000 | tf_op jit(solution)/shard_map/sort/pallas_call | solution.py:143
  19.4 1.7 %collective-permute-done.2.got_ref = f32[160,640]{1,0:T(8,128)S(1)} collective-permute-done((f32[160,640]{1,0:T(8,128)S(1)}, f32[160,640]{1,0:T(8,128)S(1)}, u32[]{:S(2)}, u32[]{:S(2)}) %collective-permute-start.2) | collective-permute-done | bytes 409632 | tf_op jit(solution)/shard_map/send2/ppermute | solution.py:323
  21.1 2.7 %collective-permute-done.refs_3_ = f32[320,640]{1,0:T(8,128)} collective-permute-done((f32[320,640]{1,0:T(8,128)S(1)}, f32[320,640]{1,0:T(8,128)}, u32[]{:S(2)}, u32[]{:S(2)}) %collective-permute-start) | collective-permute-done | bytes 819232 | tf_op jit(solution)/shard_map/send0/ppermute | solution.py:323
  23.7 5.1 %collective-permute-done.1.refs_4_ = f32[320,640]{1,0:T(8,128)} collective-permute-done((f32[320,640]{1,0:T(8,128)S(1)}, f32[320,640]{1,0:T(8,128)}, u32[]{:S(2)}, u32[]{:S(2)}) %collective-permute-start.1) | collective-permute-done | bytes 819232 | tf_op jit(solution)/shard_map/send1/ppermute | solution.py:323
  28.9 0.2 join.1.refs_0_
  29.1 0.0 copy-start.1
  29.1 0.6 collective-permute-start.5
  29.7 1.6 %collective-permute-start.3 = (f32[320,640]{1,0:T(8,128)}, f32[320,640]{1,0:T(8,128)}, u32[]{:S(2)}, u32[]{:S(2)}) collective-permute-start(f32[320,640]{1,0:T(8,128)} %collective-permute-done.refs_3_), channel_id=1, source_target_pairs={{8,16},{9,17},{10,18},{11,19},{12,20},{13,21},{14,22},{15,23},{16,... | collective-permute-start | bytes 2457608 | tf_op jit(solution)/shard_map/send3/ppermute | solution.py:323
  31.2 1.3 collective-permute-start.4
  32.5 0.6 collective-permute-start.7
  33.1 14.9 %collective-permute-done.5.refs_2_ = f32[320,640]{1,0:T(8,128)} collective-permute-done((f32[320,640]{1,0:T(8,128)S(1)}, f32[320,640]{1,0:T(8,128)}, u32[]{:S(2)}, u32[]{:S(2)}) %collective-permute-start.5) | collective-permute-done | bytes 819232 | tf_op jit(solution)/shard_map/send5/ppermute | solution.py:323
  48.0 0.0 collective-permute-done.6.refs_1_
  48.0 0.9 copy-done.3
  49.0 0.0 collective-permute-done.3
  49.0 6.6 %collective-permute-done.4 = f32[320,640]{1,0:T(8,128)} collective-permute-done((f32[320,640]{1,0:T(8,128)}, f32[320,640]{1,0:T(8,128)}, u32[]{:S(2)}, u32[]{:S(2)}) %collective-permute-start.4) | collective-permute-done | bytes 819232 | tf_op jit(solution)/shard_map/send4/ppermute | solution.py:323
  55.6 0.0 collective-permute-done.7.refs_1_
  55.6 1.3 broadcast_select_fusion.refs_5_
  56.9 1.5 collective-permute-start.9
  58.4 1.6 %collective-permute-start.10 = (f32[4,8,6400]{2,1,0:T(8,128)S(1)}, f32[4,8,6400]{2,1,0:T(8,128)S(1)}, u32[]{:S(2)}, u32[]{:S(2)}) collective-permute-start(f32[4,8,6400]{2,1,0:T(8,128)S(1)} %sort.1.refs_0_), channel_id=1, source_target_pairs={{0,2},{1,3},{2,0},{3,1},{4,6},{5,7},{6,4},{7,5},{8,10},{9,11},{10,... | collective-permute-start | bytes 2457608 | tf_op jit(solution)/shard_map/send10/ppermute | solution.py:323
  60.0 1.1 copy-done.2
  61.1 1.8 %arrange.1 = (bf16[4,320,640]{2,1,0:T(8,128)(2,1)S(1)}, bf16[4,320,640]{2,1,0:T(8,128)(2,1)S(1)}) custom-call(f32[320,640]{1,0:T(8,128)S(1)} %copy-done.2, f32[320,640]{1,0:T(8,128)S(1)} %copy-done.4, f32[320,640]{1,0:T(8,128)} %collective-permute-done.5.refs_2_, f32[320,640]{1,0:T(8,128)} %collective-permute-done.8.refs_3_), custom_call_target="tpu_custom_call" | custom-call | flops 3000000000 | bytes 9000000 | tf_op jit(solution)/shard_map/arrange/pallas_call | solution.py:143
  63.0 7.2 %cycle.2.refs_2_ = f32[640,640]{1,0:T(8,128)S(1)} custom-call(bf16[4,320,640]{2,1,0:T(8,128)(2,1)S(1)} %get-tuple-element.55.refs_0_, bf16[4,320,640]{2,1,0:T(8,128)(2,1)S(1)} %get-tuple-element.56.refs_1_, f32[320,640]{1,0:T(8,128)S(1)} %turn.1.refs_2_, f32[320,640]{1,0:T(8,128)} %collective-permute-done.refs_3_, ...), custom_call_target="tpu_custom_call" | custom-call | flops 5800000000 | bytes 17400000 | tf_op jit(solution)/shard_map/cycle/pallas_call | solution.py:143
  70.2 0.0 copy-start.14
  70.2 9.3 %collective-permute-done.9.refs_3_ = f32[320,640]{1,0:T(8,128)S(1)} collective-permute-done((f32[320,640]{1,0:T(8,128)S(1)}, f32[320,640]{1,0:T(8,128)S(1)}, u32[]{:S(2)}, u32[]{:S(2)}) %collective-permute-start.9) | collective-permute-done | bytes 819232 | tf_op jit(solution)/shard_map/send8/ppermute | solution.py:323
  79.5 0.0 collective-permute-done.10.refs_2_
  79.5 1.7 %cycle.3 = (f32[160,640]{1,0:T(8,128)S(1)}, f32[160,640]{1,0:T(8,128)S(1)}, f32[160,640]{1,0:T(8,128)S(1)}, f32[160,640]{1,0:T(8,128)S(1)}) custom-call(bf16[4,320,640]{2,1,0:T(8,128)(2,1)S(1)} %get-tuple-element.55.refs_0_, bf16[4,320,640]{2,1,0:T(8,128)(2,1)S(1)} %get-tuple-element.56.refs_1_, f32[640,640]{1,0:T(8,128)S(1)} %cycle.2.refs_2_, ...), custom_call_target="tpu_custom_call" | custom-call | flops 2200000000 | bytes 6600000 | tf_op jit(solution)/shard_map/cycle/pallas_call | solution.py:143
  81.1 0.8 copy-done.5
  81.9 0.7 copy-done.8
  82.7 0.7 copy-done.10
  83.4 0.7 copy-done.7
  84.2 0.1 copy.8.info.window
  84.3 1.5 %collective-permute-start.11 = (f32[160,640]{1,0:T(8,128)}, f32[160,640]{1,0:T(8,128)S(1)}, u32[]{:S(2)}, u32[]{:S(2)}) collective-permute-start(f32[160,640]{1,0:T(8,128)} %copy-done.7), channel_id=1, source_target_pairs={{0,4},{1,5},{2,6},{3,7},{4,0},{5,1},{6,2},{7,3},{8,12},{9,13},{10,... | collective-permute-start | bytes 1228808 | tf_op jit(solution)/shard_map/send11/ppermute | solution.py:323
  85.8 0.7 collective-permute-done.12.refs_3_
  86.5 10.8 %ladder.2 = f32[2,2,32,200]{3,2,1,0:T(8,128)S(1)} custom-call(s32[4,2]{1,0:T(4,128)S(1)} %copy.8.info.window, f32[4,8,6400]{2,1,0:T(8,128)S(1)} %sort.1.refs_0_, f32[4,8,6400]{2,1,0:T(8,128)S(1)} %collective-permute-done.7.refs_1_, f32[4,8,6400]{2,1,0:T(8,128)S(1)} %collective-permute-done.10.refs_2_, f32[4,8,6400]{2,1,0:T(8,128)S(1)} %collective-permute-done.12.refs_3_, ...), custom_call_target="tpu_custom_call" | custom-call | flops 11000000512 | bytes 33000000 | tf_op jit(solution)/shard_map/ladder/pallas_call | solution.py:118
  97.3 0.0 collective-permute-done.11.got_ref
  97.3 0.0 copy-done.6
  97.3 1.6 %collective-permute-start.13 = (f32[160,640]{1,0:T(8,128)S(1)}, f32[160,640]{1,0:T(8,128)S(1)}, u32[]{:S(2)}, u32[]{:S(2)}) collective-permute-start(f32[160,640]{1,0:T(8,128)S(1)} %copy-done.6), channel_id=1, source_target_pairs={{0,4},{1,5},{2,6},{3,7},{4,0},{5,1},{6,2},{7,3},{8,12},{9,13},{10,... | collective-permute-start | bytes 1228808 | tf_op jit(solution)/shard_map/send13/ppermute | solution.py:323
  98.9 0.9 add.8
  99.8 3.2 %collective-permute-start.14 = (f32[80,640]{1,0:T(8,128)}, f32[80,640]{1,0:T(8,128)S(1)}, u32[]{:S(2)}, u32[]{:S(2)}) collective-permute-start(f32[80,640]{1,0:T(8,128)} %get-tuple-element.81), channel_id=1, source_target_pairs={{0,0},{1,8},{2,16},{3,24},{4,4},{5,12},{6,20},{7,28},{8,1},{9,9},{... | collective-permute-start | bytes 614408 | tf_op jit(solution)/shard_map/send14/ppermute | solution.py:323
  103.0 2.5 %collective-permute-start.15 = (f32[80,640]{1,0:T(8,128)}, f32[80,640]{1,0:T(8,128)}, u32[]{:S(2)}, u32[]{:S(2)}) collective-permute-start(f32[80,640]{1,0:T(8,128)} %get-tuple-element.82), channel_id=1, source_target_pairs={{0,4},{1,12},{2,20},{3,28},{4,0},{5,8},{6,16},{7,24},{8,5},{9,13},... | collective-permute-start | bytes 614408 | tf_op jit(solution)/shard_map/send15/ppermute | solution.py:323
  105.5 10.8 %ladder.3 = f32[2,2,32,200]{3,2,1,0:T(8,128)S(1)} custom-call(s32[4,2]{1,0:T(4,128)S(1)} %copy.8.info.window, f32[4,8,6400]{2,1,0:T(8,128)S(1)} %sort.1.refs_0_, f32[4,8,6400]{2,1,0:T(8,128)S(1)} %collective-permute-done.7.refs_1_, f32[4,8,6400]{2,1,0:T(8,128)S(1)} %collective-permute-done.10.refs_2_, f32[4,8,6400]{2,1,0:T(8,128)S(1)} %collective-permute-done.12.refs_3_, ...), custom_call_target="tpu_custom_call" | custom-call | flops 11000000512 | bytes 33000000 | tf_op jit(solution)/shard_map/ladder/pallas_call | solution.py:118
  116.4 0.5 collective-permute-start.18
  117.0 0.0 collective-permute-start.19
  117.0 1.4 collective-permute-start.20
  118.4 0.1 add.9
  118.6 0.0 collective-permute-done.18
  118.6 3.4 %collective-permute-start.16 = (f32[80,640]{1,0:T(8,128)S(1)}, f32[80,640]{1,0:T(8,128)S(1)}, u32[]{:S(2)}, u32[]{:S(2)}) collective-permute-start(f32[80,640]{1,0:T(8,128)S(1)} %get-tuple-element.83), channel_id=1, source_target_pairs={{0,0},{1,8},{2,16},{3,24},{4,4},{5,12},{6,20},{7,28},{8,1},{9,9},{... | collective-permute-start | bytes 614408 | tf_op jit(solution)/shard_map/send16/ppermute | solution.py:323
  122.0 1.3 collective-permute-done.19
  123.3 2.3 %collective-permute-start.17 = (f32[80,640]{1,0:T(8,128)S(1)}, f32[80,640]{1,0:T(8,128)S(1)}, u32[]{:S(2)}, u32[]{:S(2)}) collective-permute-start(f32[80,640]{1,0:T(8,128)S(1)} %get-tuple-element.84), channel_id=1, source_target_pairs={{0,4},{1,12},{2,20},{3,28},{4,0},{5,8},{6,16},{7,24},{8,5},{9,13},... | collective-permute-start | bytes 614408 | tf_op jit(solution)/shard_map/send17/ppermute | solution.py:323
  125.7 0.1 copy.7
  125.8 0.5 reshape.14.ladder_ref
  126.3 0.0 collective-permute-done.15.c0_ref
  126.3 12.7 %collective-permute-done.16.s1_ref = f32[80,640]{1,0:T(8,128)S(1)} collective-permute-done((f32[80,640]{1,0:T(8,128)S(1)}, f32[80,640]{1,0:T(8,128)S(1)}, u32[]{:S(2)}, u32[]{:S(2)}) %collective-permute-start.16) | collective-permute-done | bytes 204832 | tf_op jit(solution)/shard_map/send16/ppermute | solution.py:323
  139.1 4.1 %collective-permute-done.17.c1_ref = f32[80,640]{1,0:T(8,128)S(1)} collective-permute-done((f32[80,640]{1,0:T(8,128)S(1)}, f32[80,640]{1,0:T(8,128)S(1)}, u32[]{:S(2)}, u32[]{:S(2)}) %collective-permute-start.17) | collective-permute-done | bytes 204832 | tf_op jit(solution)/shard_map/send17/ppermute | solution.py:323
  143.2 2.6 %merge.1 = f32[2,4,160,160]{3,2,1,0:T(8,128)S(1)} custom-call(s32[4,2]{1,0:T(4,128)S(1)} %copy.8.info.window, f32[160,640]{1,0:T(8,128)S(1)} %copy-done.13, f32[160,640]{1,0:T(8,128)S(1)} %get-tuple-element.80.one_ref, f32[80,640]{1,0:T(8,128)S(1)} %collective-permute-done.14.s0_ref, f32[80,640]{1,0:T(8,128)} %collective-permute-done.15.c0_ref, ...), custom_call_target="tpu_custom_call" | custom-call | flops 2000000000 | bytes 6000000 | tf_op jit(solution)/shard_map/merge/pallas_call | solution.py:143
  145.7 1.9 %reshape.15 = f32[2,4,25600]{2,1,0:T(4,128)} reshape(f32[2,4,160,160]{3,2,1,0:T(8,128)S(1)} %merge.1) | data formatting | bytes 1638400 | tf_op jit(solution)/shard_map/reshape | solution.py:408
  (33 shorter events, 0.2 us)
Async XLA Ops:
  2.0 6.5 %copy-start = (f32[2,4,25600]{2,1,0:T(4,128)S(1)}, f32[2,4,25600]{2,1,0:T(4,128)}, u32[]{:S(2)}) copy-start(f32[2,4,25600]{2,1,0:T(4,128)} %flat_ref) | copy-start | bytes 2457604
  2.8 21.0 %collective-permute-start = (f32[320,640]{1,0:T(8,128)S(1)}, f32[320,640]{1,0:T(8,128)}, u32[]{:S(2)}, u32[]{:S(2)}) collective-permute-start(f32[320,640]{1,0:T(8,128)S(1)} %turn.1.refs_2_), channel_id=1, source_target_pairs={{0,8},{1,9},{2,10},{3,11},{4,12},{5,13},{6,14},{7,15},{8,16},{9,17... | collective-permute-start | bytes 2457608 | tf_op jit(solution)/shard_map/send0/ppermute | solution.py:323
  7.2 21.7 %collective-permute-start.1 = (f32[320,640]{1,0:T(8,128)S(1)}, f32[320,640]{1,0:T(8,128)}, u32[]{:S(2)}, u32[]{:S(2)}) collective-permute-start(f32[320,640]{1,0:T(8,128)S(1)} %turn.1.refs_2_), channel_id=1, source_target_pairs={{8,0},{9,1},{10,2},{11,3},{12,4},{13,5},{14,6},{15,7},{16,8},{17,9... | collective-permute-start | bytes 2457608 | tf_op jit(solution)/shard_map/send1/ppermute | solution.py:323
  10.1 11.0 %collective-permute-start.2 = (f32[160,640]{1,0:T(8,128)S(1)}, f32[160,640]{1,0:T(8,128)S(1)}, u32[]{:S(2)}, u32[]{:S(2)}) collective-permute-start(f32[160,640]{1,0:T(8,128)S(1)} %get-tuple-element.48), channel_id=1, source_target_pairs={{0,4},{1,5},{2,6},{3,7},{4,0},{5,1},{6,2},{7,3},{8,12},{9,13},{10,... | collective-permute-start | bytes 1228808 | tf_op jit(solution)/shard_map/send2/ppermute | solution.py:323
  29.1 27.9 %copy-start.1 = (f32[320,640]{1,0:T(8,128)}, f32[320,640]{1,0:T(8,128)S(1)}, u32[]{:S(2)}) copy-start(f32[320,640]{1,0:T(8,128)S(1)} %join.1.refs_0_) | copy-start | bytes 2457604
  29.1 19.0 %collective-permute-start.5 = (f32[320,640]{1,0:T(8,128)S(1)}, f32[320,640]{1,0:T(8,128)}, u32[]{:S(2)}, u32[]{:S(2)}) collective-permute-start(f32[320,640]{1,0:T(8,128)S(1)} %join.1.refs_0_), channel_id=1, source_target_pairs={{0,2},{1,3},{2,0},{3,1},{4,6},{5,7},{6,4},{7,5},{8,10},{9,11},{10,... | collective-permute-start | bytes 2457608 | tf_op jit(solution)/shard_map/send5/ppermute | solution.py:323
  29.7 18.4 %collective-permute-start.6 = (f32[320,640]{1,0:T(8,128)S(1)}, f32[320,640]{1,0:T(8,128)S(1)}, u32[]{:S(2)}, u32[]{:S(2)}) collective-permute-start(f32[320,640]{1,0:T(8,128)S(1)} %join.1.refs_0_), channel_id=1, source_target_pairs={{0,1},{1,0},{2,3},{3,2},{4,5},{5,4},{6,7},{7,6},{8,9},{9,8},{10,11... | collective-permute-start | bytes 2457608 | tf_op jit(solution)/shard_map/send6/ppermute | solution.py:323
  29.7 19.3 %collective-permute-start.3 = (f32[320,640]{1,0:T(8,128)}, f32[320,640]{1,0:T(8,128)}, u32[]{:S(2)}, u32[]{:S(2)}) collective-permute-start(f32[320,640]{1,0:T(8,128)} %collective-permute-done.refs_3_), channel_id=1, source_target_pairs={{8,16},{9,17},{10,18},{11,19},{12,20},{13,21},{14,22},{15,23},{16,... | collective-permute-start | bytes 2457608 | tf_op jit(solution)/shard_map/send3/ppermute | solution.py:323
  31.2 24.3 %collective-permute-start.4 = (f32[320,640]{1,0:T(8,128)}, f32[320,640]{1,0:T(8,128)}, u32[]{:S(2)}, u32[]{:S(2)}) collective-permute-start(f32[320,640]{1,0:T(8,128)} %collective-permute-done.1.refs_4_), channel_id=1, source_target_pairs={{8,0},{9,1},{10,2},{11,3},{12,4},{13,5},{14,6},{15,7},{16,8},{17,9... | collective-permute-start | bytes 2457608 | tf_op jit(solution)/shard_map/send4/ppermute | solution.py:323
  32.5 23.1 %collective-permute-start.7 = (f32[4,8,6400]{2,1,0:T(8,128)S(1)}, f32[4,8,6400]{2,1,0:T(8,128)S(1)}, u32[]{:S(2)}, u32[]{:S(2)}) collective-permute-start(f32[4,8,6400]{2,1,0:T(8,128)S(1)} %sort.1.refs_0_), channel_id=1, source_target_pairs={{0,1},{1,0},{2,3},{3,2},{4,5},{5,4},{6,7},{7,6},{8,9},{9,8},{10,11... | collective-permute-start | bytes 2457608 | tf_op jit(solution)/shard_map/send7/ppermute | solution.py:323
  48.0 0.9 copy-start.3
  55.6 4.4 %collective-permute-start.8 = (f32[320,640]{1,0:T(8,128)}, f32[320,640]{1,0:T(8,128)}, u32[]{:S(2)}, u32[]{:S(2)}) collective-permute-start(f32[320,640]{1,0:T(8,128)} %collective-permute-done.5.refs_2_), channel_id=1, source_target_pairs={{0,1},{1,0},{2,3},{3,2},{4,5},{5,4},{6,7},{7,6},{8,9},{9,8},{10,11... | collective-permute-start | bytes 2457608 | tf_op jit(solution)/shard_map/send9/ppermute | solution.py:323
  55.6 4.4 %copy-start.4 = (f32[320,640]{1,0:T(8,128)S(1)}, f32[320,640]{1,0:T(8,128)}, u32[]{:S(2)}) copy-start(f32[320,640]{1,0:T(8,128)} %copy-done.3) | copy-start | bytes 2457604
  56.9 22.5 %collective-permute-start.9 = (f32[320,640]{1,0:T(8,128)S(1)}, f32[320,640]{1,0:T(8,128)S(1)}, u32[]{:S(2)}, u32[]{:S(2)}) collective-permute-start(f32[320,640]{1,0:T(8,128)S(1)} %broadcast_select_fusion.refs_5_), channel_id=1, source_target_pairs={{8,0},{9,1},{10,2},{11,3},{12,4},{13,5},{14,6},{15,7},{16,24},{17,... | collective-permute-start | bytes 2457608 | tf_op jit(solution)/shard_map/send8/ppermute | solution.py:323
  58.4 21.1 %collective-permute-start.10 = (f32[4,8,6400]{2,1,0:T(8,128)S(1)}, f32[4,8,6400]{2,1,0:T(8,128)S(1)}, u32[]{:S(2)}, u32[]{:S(2)}) collective-permute-start(f32[4,8,6400]{2,1,0:T(8,128)S(1)} %sort.1.refs_0_), channel_id=1, source_target_pairs={{0,2},{1,3},{2,0},{3,1},{4,6},{5,7},{6,4},{7,5},{8,10},{9,11},{10,... | collective-permute-start | bytes 2457608 | tf_op jit(solution)/shard_map/send10/ppermute | solution.py:323
  60.0 1.1 copy-start.2
  70.2 14.0 %copy-start.14 = (s32[4,2]{0,1:T(2,128)S(1)}, s32[4,2]{0,1:T(2,128)}, u32[]{:S(2)}) copy-start(s32[4,2]{0,1:T(2,128)} %param.7) | copy-start | bytes 100
  81.1 0.8 copy-start.5
  81.9 0.7 copy-start.8
  82.7 0.8 copy-start.10
  83.4 0.7 copy-start.7
  84.2 2.3 %collective-permute-start.12 = (f32[4,8,6400]{2,1,0:T(8,128)S(1)}, f32[4,8,6400]{2,1,0:T(8,128)S(1)}, u32[]{:S(2)}, u32[]{:S(2)}) collective-permute-start(f32[4,8,6400]{2,1,0:T(8,128)S(1)} %collective-permute-done.10.refs_2_), channel_id=1, source_target_pairs={{0,1},{1,0},{2,3},{3,2},{4,5},{5,4},{6,7},{7,6},{8,9},{9,8},{10,11... | collective-permute-start | bytes 2457608 | tf_op jit(solution)/shard_map/send12/ppermute | solution.py:323
  84.2 13.0 %copy-start.6 = (f32[160,640]{1,0:T(8,128)S(1)}, f32[160,640]{1,0:T(8,128)}, u32[]{:S(2)}) copy-start(f32[160,640]{1,0:T(8,128)} %copy-done.5) | copy-start | bytes 1228804
  84.3 14.6 %copy-start.11 = (f32[160,640]{1,0:T(8,128)S(1)}, f32[160,640]{1,0:T(8,128)}, u32[]{:S(2)}) copy-start(f32[160,640]{1,0:T(8,128)} %copy-done.10) | copy-start | bytes 1228804
  84.3 13.0 %collective-permute-start.11 = (f32[160,640]{1,0:T(8,128)}, f32[160,640]{1,0:T(8,128)S(1)}, u32[]{:S(2)}, u32[]{:S(2)}) collective-permute-start(f32[160,640]{1,0:T(8,128)} %copy-done.7), channel_id=1, source_target_pairs={{0,4},{1,5},{2,6},{3,7},{4,0},{5,1},{6,2},{7,3},{8,12},{9,13},{10,... | collective-permute-start | bytes 1228808 | tf_op jit(solution)/shard_map/send11/ppermute | solution.py:323
  97.3 19.1 %collective-permute-start.13 = (f32[160,640]{1,0:T(8,128)S(1)}, f32[160,640]{1,0:T(8,128)S(1)}, u32[]{:S(2)}, u32[]{:S(2)}) collective-permute-start(f32[160,640]{1,0:T(8,128)S(1)} %copy-done.6), channel_id=1, source_target_pairs={{0,4},{1,5},{2,6},{3,7},{4,0},{5,1},{6,2},{7,3},{8,12},{9,13},{10,... | collective-permute-start | bytes 1228808 | tf_op jit(solution)/shard_map/send13/ppermute | solution.py:323
  99.8 16.6 %copy-start.12 = (f32[160,640]{1,0:T(8,128)}, f32[160,640]{1,0:T(8,128)S(1)}, u32[]{:S(2)}) copy-start(f32[160,640]{1,0:T(8,128)S(1)} %get-tuple-element.72.zero_ref) | copy-start | bytes 1228804
  99.8 26.5 %collective-permute-start.14 = (f32[80,640]{1,0:T(8,128)}, f32[80,640]{1,0:T(8,128)S(1)}, u32[]{:S(2)}, u32[]{:S(2)}) collective-permute-start(f32[80,640]{1,0:T(8,128)} %get-tuple-element.81), channel_id=1, source_target_pairs={{0,0},{1,8},{2,16},{3,24},{4,4},{5,12},{6,20},{7,28},{8,1},{9,9},{... | collective-permute-start | bytes 614408 | tf_op jit(solution)/shard_map/send14/ppermute | solution.py:323
  103.0 15.4 %copy-start.9 = (f32[160,640]{1,0:T(8,128)S(1)}, f32[160,640]{1,0:T(8,128)}, u32[]{:S(2)}) copy-start(f32[160,640]{1,0:T(8,128)} %copy-done.8) | copy-start | bytes 1228804
  103.0 23.3 %collective-permute-start.15 = (f32[80,640]{1,0:T(8,128)}, f32[80,640]{1,0:T(8,128)}, u32[]{:S(2)}, u32[]{:S(2)}) collective-permute-start(f32[80,640]{1,0:T(8,128)} %get-tuple-element.82), channel_id=1, source_target_pairs={{0,4},{1,12},{2,20},{3,28},{4,0},{5,8},{6,16},{7,24},{8,5},{9,13},... | collective-permute-start | bytes 614408 | tf_op jit(solution)/shard_map/send15/ppermute | solution.py:323
  116.4 2.1 %collective-permute-start.18 = (f32[4,2,8,200]{3,2,1,0:T(8,128)S(1)}, f32[4,2,8,200]{3,2,1,0:T(8,128)S(1)}, u32[]{:S(2)}, u32[]{:S(2)}) collective-permute-start(f32[4,2,8,200]{3,2,1,0:T(8,128)S(1)} %get-tuple-element.92), channel_id=1, source_target_pairs={{0,1},{1,0},{2,3},{3,2},{4,5},{5,4},{6,7},{7,6},{8,9},{9,8},{10,11... | collective-permute-start | bytes 153608 | tf_op jit(solution)/shard_map/send18/ppermute | solution.py:323
  117.0 6.3 %collective-permute-start.19 = (f32[4,2,8,200]{3,2,1,0:T(8,128)S(1)}, f32[4,2,8,200]{3,2,1,0:T(8,128)S(1)}, u32[]{:S(2)}, u32[]{:S(2)}) collective-permute-start(f32[4,2,8,200]{3,2,1,0:T(8,128)S(1)} %get-tuple-element.91), channel_id=1, source_target_pairs={{0,2},{1,3},{2,0},{3,1},{4,6},{5,7},{6,4},{7,5},{8,10},{9,11},{10,... | collective-permute-start | bytes 153608 | tf_op jit(solution)/shard_map/send19/ppermute | solution.py:323
  117.0 8.6 %collective-permute-start.20 = (f32[4,2,8,200]{3,2,1,0:T(8,128)S(1)}, f32[4,2,8,200]{3,2,1,0:T(8,128)S(1)}, u32[]{:S(2)}, u32[]{:S(2)}) collective-permute-start(f32[4,2,8,200]{3,2,1,0:T(8,128)S(1)} %get-tuple-element.90), channel_id=1, source_target_pairs={{0,3},{1,2},{2,1},{3,0},{4,7},{5,6},{6,5},{7,4},{8,11},{9,10},{10,... | collective-permute-start | bytes 153608 | tf_op jit(solution)/shard_map/send20/ppermute | solution.py:323
  118.6 20.5 %collective-permute-start.16 = (f32[80,640]{1,0:T(8,128)S(1)}, f32[80,640]{1,0:T(8,128)S(1)}, u32[]{:S(2)}, u32[]{:S(2)}) collective-permute-start(f32[80,640]{1,0:T(8,128)S(1)} %get-tuple-element.83), channel_id=1, source_target_pairs={{0,0},{1,8},{2,16},{3,24},{4,4},{5,12},{6,20},{7,28},{8,1},{9,9},{... | collective-permute-start | bytes 614408 | tf_op jit(solution)/shard_map/send16/ppermute | solution.py:323
  123.3 19.9 %collective-permute-start.17 = (f32[80,640]{1,0:T(8,128)S(1)}, f32[80,640]{1,0:T(8,128)S(1)}, u32[]{:S(2)}, u32[]{:S(2)}) collective-permute-start(f32[80,640]{1,0:T(8,128)S(1)} %get-tuple-element.84), channel_id=1, source_target_pairs={{0,4},{1,12},{2,20},{3,28},{4,0},{5,8},{6,16},{7,24},{8,5},{9,13},... | collective-permute-start | bytes 614408 | tf_op jit(solution)/shard_map/send17/ppermute | solution.py:323
  125.6 17.6 %copy-start.13 = (f32[160,640]{1,0:T(8,128)S(1)}, f32[160,640]{1,0:T(8,128)}, u32[]{:S(2)}) copy-start(f32[160,640]{1,0:T(8,128)} %copy-done.12) | copy-start | bytes 1228804

commit v2 on v1

--- a/solution.py
+++ b/solution.py
@@ -355,21 +355,23 @@
     a1, b1 = up(x0, (0, 1, 2)), down(x0, (1, 2, 3))
     amplitudes, x0 = after((amplitudes, x0))
     keep, give = whole(pair_kernel, "pair", 1.5, [slab] * 2, (amplitudes.reshape(four),))
+    amplitudes, give = after((amplitudes, give))
     got = swap_y(give)
     (kinds,) = whole(
-        sort_kernel, "sort", 8, [(NIRR, rows_i * cols_j, flat // NIRR)], (amplitudes,)
+        sort_kernel, "sort", 30, [(NIRR, rows_i * cols_j, flat // NIRR)], (amplitudes,)
     )
+    kinds_x, kinds_k = swap_x(kinds), swap(kinds)
     a1, b1, got, kinds = after((a1, b1, got, kinds))
 
     a2, b2 = up(a1, (1, 2)), down(b1, (1, 2))
     (u,) = whole(join_kernel, "join", 1, [(rows_i * v, cols_j * v)], (keep, got))
     u_x, u_k = swap_x(u), swap(u)
-    kinds_k = swap(kinds)
-    a2, b2, u_x, u_k, kinds, kinds_k = after((a2, b2, u_x, u_k, kinds, kinds_k))
+    a2, b2, u_k, kinds_x = after((a2, b2, u_k, kinds_x))
 
     c2 = jnp.where(lax.axis_index("row") < 4, b2, a2)
     c3 = ends(c2)
-    u_xk, kinds_x = swap(u_x), swap_x(kinds)
+    u_xk = swap(u_x)
+    all_kinds = (kinds, kinds_k, kinds_x, swap(kinds_x))
     high, low = whole(
         arrange_kernel,
         "arrange",
@@ -380,23 +382,22 @@
         jnp.bfloat16,
     )
     (part,) = cycle_part(high, low, products(x0, a1, b1, c2), None, False)
-    c3, part, kinds_x = after((c3, part, kinds_x))
+    first = ladder_of(0, 1)
+    c3, part, first, all_kinds = after((c3, part, first, all_kinds))
 
     keep0, give0, keep1, give1 = cycle_part(high, low, [("three", [c3])], part, True)
-    give0, give1, kinds_x = after((give0, give1, kinds_x))
     got0 = swap_y(give0)
-    all_kinds = (kinds, kinds_k, kinds_x, swap(kinds_x))
-    early = ladder_of(0, 2)
+    early = ladder_of(1, 2)
     got0, early, all_kinds, give1 = after((got0, early, all_kinds, give1))
 
     total0, same0, cross0 = add(keep0, got0)
     got1 = swap_y(give1)
     same0, cross0 = image(same0), image_y(cross0)
-    late = ladder_of(2, 2)
+    late = ladder_of(3, 1)
     got1, late = after((got1, late))
     total1, same1, cross1 = add(keep1, got1)
     same1, cross1 = image(same1), image_y(cross1)
-    ladder = returned(jnp.concatenate([early, late]))
+    ladder = returned(jnp.concatenate([first, early, late]))
     (merged,) = whole(
         merge_kernel,
         "merge",

time: 148 us -> 142 us (0.959)
  waiting for transfers between devices: 59.2 us -> 54.2 us
  local copies, waits for them, and re-layouts: 10.5 us -> 7.98 us
  Pallas kernels: 45.4 us -> 47.6 us
    ppermute x21, waiting for transfers between devices: 59.2 us -> 54.2 us  [send(): return lax.ppermute(a, AXES, permutation(rule))]
    unnamed x32 -> x23, local copies, waits for them, and re-layouts: 5.2 us -> 2.67 us
    pallas_call x2 -> x3, Pallas kernels: 21.6 us -> 23.8 us  [ladder_part(): pl.pallas_call(ladder_kernel, out_shape=jax.ShapeDtypeStruct((count, pair...]
  transfers between devices with their start and end apart: 21 -> 21, of which waited for: 10 -> 11; matrix products, arithmetic and copies ran while one was open for 2% -> 2% of each run, Pallas kernels for 27% -> 30%
where the time goes in v2:
time: 142 us; the launch traced here: 141 us
  waiting for transfers between devices  54.2 us (38%)
  Pallas kernels  47.6 us (34%)
  starting transfers between devices  29.9 us (21%)
  local copies, waits for them, and re-layouts  7.98 us (6%)
    ppermute x21, waiting for transfers between devices, send(): return lax.ppermute(a, AXES, permutation(rule))  54.2 us
    ppermute x21, starting transfers between devices, send(): return lax.ppermute(a, AXES, permutation(rule))  29.9 us
    pallas_call x10, Pallas kernels, whole(): pl.pallas_call(kernel, out_shape=[jax.ShapeDtypeStruct(shape, dtype) for...  23.8 us
    pallas_call x3, Pallas kernels, ladder_part(): pl.pallas_call(ladder_kernel, out_shape=jax.ShapeDtypeStruct((count, pair...  23.8 us
  transfers between devices with their start and end apart: 21, of which 11 were waited for; matrix products, arithmetic and copies ran while one was open for 2% of the time, Pallas kernels for 30%

profile of v2, /device:TPU:2, one launch (start us, length us, event | category | flops | bytes accessed | tf_op | source)
XLA Modules:
  0.0 141.3 jit_solution(12053237356685008785)
XLA Ops:
  0.0 2.0 %reshape.12.four_ref = f32[2,4,160,160]{3,2,1,0:T(8,128)S(1)} reshape(f32[2,4,25600]{2,1,0:T(4,128)} %param.5) | data formatting | bytes 1638400 | tf_op jit(solution)/shard_map/reshape | solution.py:354
  2.0 0.0 copy-start
  2.0 0.8 turn.1.refs_2_
  2.8 4.4 %collective-permute-start = (f32[320,640]{1,0:T(8,128)S(1)}, f32[320,640]{1,0:T(8,128)}, u32[]{:S(2)}, u32[]{:S(2)}) collective-permute-start(f32[320,640]{1,0:T(8,128)S(1)} %turn.1.refs_2_), channel_id=1, source_target_pairs={{0,8},{1,9},{2,10},{3,11},{4,12},{5,13},{6,14},{7,15},{8,16},{9,17... | collective-permute-start | bytes 2457608 | tf_op jit(solution)/shard_map/send0/ppermute | solution.py:323
  7.2 1.3 collective-permute-start.1
  8.5 0.8 reshape.13.four_ref
  9.3 0.8 pair.1
  10.1 1.6 %collective-permute-start.2 = (f32[160,640]{1,0:T(8,128)S(1)}, f32[160,640]{1,0:T(8,128)S(1)}, u32[]{:S(2)}, u32[]{:S(2)}) collective-permute-start(f32[160,640]{1,0:T(8,128)S(1)} %get-tuple-element.50), channel_id=1, source_target_pairs={{0,4},{1,5},{2,6},{3,7},{4,0},{5,1},{6,2},{7,3},{8,12},{9,13},{10,... | collective-permute-start | bytes 1228808 | tf_op jit(solution)/shard_map/send2/ppermute | solution.py:323
  11.7 7.7 %sort.1.refs_0_ = f32[4,8,6400]{2,1,0:T(8,128)S(1)} custom-call(f32[2,4,25600]{2,1,0:T(4,128)S(1)} %copy-done), custom_call_target="tpu_custom_call" | custom-call | flops 30000001024 | bytes 90000000 | tf_op jit(solution)/shard_map/sort/pallas_call | solution.py:143
  19.4 0.6 collective-permute-start.6
  20.0 1.1 collective-permute-done.2.got_ref
  21.1 2.7 %collective-permute-done.refs_3_ = f32[320,640]{1,0:T(8,128)} collective-permute-done((f32[320,640]{1,0:T(8,128)S(1)}, f32[320,640]{1,0:T(8,128)}, u32[]{:S(2)}, u32[]{:S(2)}) %collective-permute-start) | collective-permute-done | bytes 819232 | tf_op jit(solution)/shard_map/send0/ppermute | solution.py:323
  23.7 5.1 %collective-permute-done.1.refs_4_ = f32[320,640]{1,0:T(8,128)} collective-permute-done((f32[320,640]{1,0:T(8,128)S(1)}, f32[320,640]{1,0:T(8,128)}, u32[]{:S(2)}, u32[]{:S(2)}) %collective-permute-start.1) | collective-permute-done | bytes 819232 | tf_op jit(solution)/shard_map/send1/ppermute | solution.py:323
  28.9 1.6 %collective-permute-start.3 = (f32[320,640]{1,0:T(8,128)}, f32[320,640]{1,0:T(8,128)}, u32[]{:S(2)}, u32[]{:S(2)}) collective-permute-start(f32[320,640]{1,0:T(8,128)} %collective-permute-done.refs_3_), channel_id=1, source_target_pairs={{8,16},{9,17},{10,18},{11,19},{12,20},{13,21},{14,22},{15,23},{16,... | collective-permute-start | bytes 2457608 | tf_op jit(solution)/shard_map/send5/ppermute | solution.py:323
  30.4 1.3 collective-permute-start.4
  31.7 0.0 copy-start.9
  31.7 0.2 join.1.refs_0_
  32.0 0.1 collective-permute-start.5
  32.0 0.6 collective-permute-start.7
  32.6 0.9 copy-done.3
  33.5 7.1 %collective-permute-done.6.refs_2_ = f32[4,8,6400]{2,1,0:T(8,128)S(1)} collective-permute-done((f32[4,8,6400]{2,1,0:T(8,128)S(1)}, f32[4,8,6400]{2,1,0:T(8,128)S(1)}, u32[]{:S(2)}, u32[]{:S(2)}) %collective-permute-start.6) | collective-permute-done | bytes 819232 | tf_op jit(solution)/shard_map/send3/ppermute | solution.py:323
  40.6 0.0 collective-permute-start.10
  40.6 0.0 collective-permute-done.3
  40.6 12.3 %collective-permute-done.4 = f32[320,640]{1,0:T(8,128)} collective-permute-done((f32[320,640]{1,0:T(8,128)}, f32[320,640]{1,0:T(8,128)}, u32[]{:S(2)}, u32[]{:S(2)}) %collective-permute-start.4) | collective-permute-done | bytes 819232 | tf_op jit(solution)/shard_map/send6/ppermute | solution.py:323
  52.9 0.0 collective-permute-done.5.refs_1_
  52.9 0.9 copy-done.5
  53.8 0.0 collective-permute-start.11
  53.8 2.7 %collective-permute-done.7.refs_2_ = f32[320,640]{1,0:T(8,128)} collective-permute-done((f32[320,640]{1,0:T(8,128)S(1)}, f32[320,640]{1,0:T(8,128)}, u32[]{:S(2)}, u32[]{:S(2)}) %collective-permute-start.7) | collective-permute-done | bytes 819232 | tf_op jit(solution)/shard_map/send7/ppermute | solution.py:323
  56.5 0.0 collective-permute-start.8
  56.5 0.1 copy.9.info.window
  56.6 1.2 broadcast_select_fusion.refs_5_
  57.9 0.0 copy-start.4
  57.9 1.6 %collective-permute-start.9 = (f32[320,640]{1,0:T(8,128)S(1)}, f32[320,640]{1,0:T(8,128)S(1)}, u32[]{:S(2)}, u32[]{:S(2)}) collective-permute-start(f32[320,640]{1,0:T(8,128)S(1)} %broadcast_select_fusion.refs_5_), channel_id=1, source_target_pairs={{8,0},{9,1},{10,2},{11,3},{12,4},{13,5},{14,6},{15,7},{16,24},{17,... | collective-permute-start | bytes 2457608 | tf_op jit(solution)/shard_map/send9/ppermute | solution.py:323
  59.5 0.0 collective-permute-done.11.refs_3_
  59.5 6.5 %ladder.3 = f32[1,2,32,200]{3,2,1,0:T(8,128)S(1)} custom-call(s32[4,2]{1,0:T(4,128)S(1)} %copy.9.info.window, f32[4,8,6400]{2,1,0:T(8,128)S(1)} %sort.1.refs_0_, f32[4,8,6400]{2,1,0:T(8,128)S(1)} %collective-permute-done.10.refs_1_, f32[4,8,6400]{2,1,0:T(8,128)S(1)} %collective-permute-done.6.refs_2_, f32[4,8,6400]{2,1,0:T(8,128)S(1)} %collective-permute-done.11.refs_3_, ...), custom_call_target="tpu_custom_call" | custom-call | flops 5500000256 | bytes 16500000 | tf_op jit(solution)/shard_map/ladder/pallas_call | solution.py:118
  66.0 1.9 %arrange.1 = (bf16[4,320,640]{2,1,0:T(8,128)(2,1)S(1)}, bf16[4,320,640]{2,1,0:T(8,128)(2,1)S(1)}) custom-call(f32[320,640]{1,0:T(8,128)S(1)} %copy-done.4, f32[320,640]{1,0:T(8,128)S(1)} %copy-done.6, f32[320,640]{1,0:T(8,128)} %collective-permute-done.7.refs_2_, f32[320,640]{1,0:T(8,128)} %collective-permute-done.8.refs_3_), custom_call_target="tpu_custom_call" | custom-call | flops 3000000000 | bytes 9000000 | tf_op jit(solution)/shard_map/arrange/pallas_call | solution.py:143
  68.0 7.2 %cycle.2.refs_2_ = f32[640,640]{1,0:T(8,128)S(1)} custom-call(bf16[4,320,640]{2,1,0:T(8,128)(2,1)S(1)} %get-tuple-element.56.refs_0_, bf16[4,320,640]{2,1,0:T(8,128)(2,1)S(1)} %get-tuple-element.57.refs_1_, f32[320,640]{1,0:T(8,128)S(1)} %copy-done.2, f32[320,640]{1,0:T(8,128)} %collective-permute-done.refs_3_, f32[320,640]{1,0:T(8,128)} %collective-permute-done.1.refs_4_, ...), custom_call_target="tpu_custom_call" | custom-call | flops 5800000000 | bytes 17400000 | tf_op jit(solution)/shard_map/cycle/pallas_call | solution.py:143
  75.2 5.4 %collective-permute-done.9.refs_3_ = f32[320,640]{1,0:T(8,128)S(1)} collective-permute-done((f32[320,640]{1,0:T(8,128)S(1)}, f32[320,640]{1,0:T(8,128)S(1)}, u32[]{:S(2)}, u32[]{:S(2)}) %collective-permute-start.9) | collective-permute-done | bytes 819232 | tf_op jit(solution)/shard_map/send9/ppermute | solution.py:323
  80.6 1.7 %cycle.3 = (f32[160,640]{1,0:T(8,128)S(1)}, f32[160,640]{1,0:T(8,128)S(1)}, f32[160,640]{1,0:T(8,128)S(1)}, f32[160,640]{1,0:T(8,128)S(1)}) custom-call(bf16[4,320,640]{2,1,0:T(8,128)(2,1)S(1)} %get-tuple-element.56.refs_0_, bf16[4,320,640]{2,1,0:T(8,128)(2,1)S(1)} %get-tuple-element.57.refs_1_, f32[640,640]{1,0:T(8,128)S(1)} %cycle.2.refs_2_, ...), custom_call_target="tpu_custom_call" | custom-call | flops 2200000000 | bytes 6600000 | tf_op jit(solution)/shard_map/cycle/pallas_call | solution.py:143
  82.2 0.6 collective-permute-start.12
  82.8 10.8 %ladder.4 = f32[2,2,32,200]{3,2,1,0:T(8,128)S(1)} custom-call(s32[4,2]{1,0:T(4,128)S(1)} %copy.9.info.window, f32[4,8,6400]{2,1,0:T(8,128)S(1)} %sort.1.refs_0_, f32[4,8,6400]{2,1,0:T(8,128)S(1)} %collective-permute-done.10.refs_1_, f32[4,8,6400]{2,1,0:T(8,128)S(1)} %collective-permute-done.6.refs_2_, f32[4,8,6400]{2,1,0:T(8,128)S(1)} %collective-permute-done.11.refs_3_, ...), custom_call_target="tpu_custom_call" | custom-call | flops 11000000512 | bytes 33000000 | tf_op jit(solution)/shard_map/ladder/pallas_call | solution.py:118
  93.6 1.6 %collective-permute-start.13 = (f32[160,640]{1,0:T(8,128)S(1)}, f32[160,640]{1,0:T(8,128)S(1)}, u32[]{:S(2)}, u32[]{:S(2)}) collective-permute-start(f32[160,640]{1,0:T(8,128)S(1)} %get-tuple-element.75), channel_id=1, source_target_pairs={{0,4},{1,5},{2,6},{3,7},{4,0},{5,1},{6,2},{7,3},{8,12},{9,13},{10,... | collective-permute-start | bytes 1228808 | tf_op jit(solution)/shard_map/send13/ppermute | solution.py:323
  95.2 0.9 add.8
  96.1 0.7 copy-done.7
  96.9 4.5 %collective-permute-start.14 = (f32[80,640]{1,0:T(8,128)}, f32[80,640]{1,0:T(8,128)S(1)}, u32[]{:S(2)}, u32[]{:S(2)}) collective-permute-start(f32[80,640]{1,0:T(8,128)} %get-tuple-element.82), channel_id=1, source_target_pairs={{0,0},{1,8},{2,16},{3,24},{4,4},{5,12},{6,20},{7,28},{8,1},{9,9},{... | collective-permute-start | bytes 614408 | tf_op jit(solution)/shard_map/send14/ppermute | solution.py:323
  101.4 1.4 collective-permute-start.15
  102.8 6.5 %ladder.5 = f32[1,2,32,200]{3,2,1,0:T(8,128)S(1)} custom-call(s32[4,2]{1,0:T(4,128)S(1)} %copy.9.info.window, f32[4,8,6400]{2,1,0:T(8,128)S(1)} %sort.1.refs_0_, f32[4,8,6400]{2,1,0:T(8,128)S(1)} %collective-permute-done.10.refs_1_, f32[4,8,6400]{2,1,0:T(8,128)S(1)} %collective-permute-done.6.refs_2_, f32[4,8,6400]{2,1,0:T(8,128)S(1)} %collective-permute-done.11.refs_3_, ...), custom_call_target="tpu_custom_call" | custom-call | flops 5500000256 | bytes 16500000 | tf_op jit(solution)/shard_map/ladder/pallas_call | solution.py:118
  109.3 0.0 collective-permute-done.13.got_ref
  109.4 0.1 collective-permute-start.20
  109.5 2.3 %collective-permute-start.19 = (f32[4,2,8,200]{3,2,1,0:T(8,128)S(1)}, f32[4,2,8,200]{3,2,1,0:T(8,128)S(1)}, u32[]{:S(2)}, u32[]{:S(2)}) collective-permute-start(f32[4,2,8,200]{3,2,1,0:T(8,128)S(1)} %get-tuple-element.93), channel_id=1, source_target_pairs={{0,2},{1,3},{2,0},{3,1},{4,6},{5,7},{6,4},{7,5},{8,10},{9,11},{10,... | collective-permute-start | bytes 153608 | tf_op jit(solution)/shard_map/send19/ppermute | solution.py:323
  111.8 0.0 collective-permute-start.18
  111.8 0.1 add.9
  111.9 2.5 %collective-permute-done.20 = f32[4,2,8,200]{3,2,1,0:T(8,128)S(1)} collective-permute-done((f32[4,2,8,200]{3,2,1,0:T(8,128)S(1)}, f32[4,2,8,200]{3,2,1,0:T(8,128)S(1)}, u32[]{:S(2)}, u32[]{:S(2)}) %collective-permute-start.20) | collective-permute-done | bytes 51232 | tf_op jit(solution)/shard_map/send20/ppermute | solution.py:323
  114.4 3.2 %collective-permute-start.16 = (f32[80,640]{1,0:T(8,128)S(1)}, f32[80,640]{1,0:T(8,128)S(1)}, u32[]{:S(2)}, u32[]{:S(2)}) collective-permute-start(f32[80,640]{1,0:T(8,128)S(1)} %get-tuple-element.84), channel_id=1, source_target_pairs={{0,0},{1,8},{2,16},{3,24},{4,4},{5,12},{6,20},{7,28},{8,1},{9,9},{... | collective-permute-start | bytes 614408 | tf_op jit(solution)/shard_map/send16/ppermute | solution.py:323
  117.6 0.5 collective-permute-done.19
  118.0 3.2 %collective-permute-start.17 = (f32[80,640]{1,0:T(8,128)S(1)}, f32[80,640]{1,0:T(8,128)S(1)}, u32[]{:S(2)}, u32[]{:S(2)}) collective-permute-start(f32[80,640]{1,0:T(8,128)S(1)} %get-tuple-element.85), channel_id=1, source_target_pairs={{0,4},{1,12},{2,20},{3,28},{4,0},{5,8},{6,16},{7,24},{8,5},{9,13},... | collective-permute-start | bytes 614408 | tf_op jit(solution)/shard_map/send17/ppermute | solution.py:323
  121.2 0.0 collective-permute-done.18
  121.3 0.1 copy.8
  121.5 0.5 reshape.14.ladder_ref
  122.0 0.0 collective-permute-done.14.s0_ref
  122.0 12.6 %collective-permute-done.16.s1_ref = f32[80,640]{1,0:T(8,128)S(1)} collective-permute-done((f32[80,640]{1,0:T(8,128)S(1)}, f32[80,640]{1,0:T(8,128)S(1)}, u32[]{:S(2)}, u32[]{:S(2)}) %collective-permute-start.16) | collective-permute-done | bytes 204832 | tf_op jit(solution)/shard_map/send16/ppermute | solution.py:323
  134.5 2.4 %collective-permute-done.17.c1_ref = f32[80,640]{1,0:T(8,128)S(1)} collective-permute-done((f32[80,640]{1,0:T(8,128)S(1)}, f32[80,640]{1,0:T(8,128)S(1)}, u32[]{:S(2)}, u32[]{:S(2)}) %collective-permute-start.17) | collective-permute-done | bytes 204832 | tf_op jit(solution)/shard_map/send17/ppermute | solution.py:323
  136.9 2.6 %merge.1 = f32[2,4,160,160]{3,2,1,0:T(8,128)S(1)} custom-call(s32[4,2]{1,0:T(4,128)S(1)} %copy.9.info.window, f32[160,640]{1,0:T(8,128)S(1)} %copy-done.8, f32[160,640]{1,0:T(8,128)S(1)} %get-tuple-element.81.one_ref, f32[80,640]{1,0:T(8,128)S(1)} %collective-permute-done.14.s0_ref, f32[80,640]{1,0:T(8,128)} %collective-permute-done.15.c0_ref, ...), custom_call_target="tpu_custom_call" | custom-call | flops 2000000000 | bytes 6000000 | tf_op jit(solution)/shard_map/merge/pallas_call | solution.py:143
  139.5 1.9 %reshape.15 = f32[2,4,25600]{2,1,0:T(4,128)} reshape(f32[2,4,160,160]{3,2,1,0:T(8,128)S(1)} %merge.1) | data formatting | bytes 1638400 | tf_op jit(solution)/shard_map/reshape | solution.py:409
  (25 shorter events, 0.2 us)
Async XLA Ops:
  2.0 6.5 %copy-start = (f32[2,4,25600]{2,1,0:T(4,128)S(1)}, f32[2,4,25600]{2,1,0:T(4,128)}, u32[]{:S(2)}) copy-start(f32[2,4,25600]{2,1,0:T(4,128)} %flat_ref) | copy-start | bytes 2457604
  2.8 7.3 %copy-start.1 = (f32[320,640]{1,0:T(8,128)}, f32[320,640]{1,0:T(8,128)S(1)}, u32[]{:S(2)}) copy-start(f32[320,640]{1,0:T(8,128)S(1)} %turn.1.refs_2_) | copy-start | bytes 2457604
  2.8 21.0 %collective-permute-start = (f32[320,640]{1,0:T(8,128)S(1)}, f32[320,640]{1,0:T(8,128)}, u32[]{:S(2)}, u32[]{:S(2)}) collective-permute-start(f32[320,640]{1,0:T(8,128)S(1)} %turn.1.refs_2_), channel_id=1, source_target_pairs={{0,8},{1,9},{2,10},{3,11},{4,12},{5,13},{6,14},{7,15},{8,16},{9,17... | collective-permute-start | bytes 2457608 | tf_op jit(solution)/shard_map/send0/ppermute | solution.py:323
  7.2 21.7 %collective-permute-start.1 = (f32[320,640]{1,0:T(8,128)S(1)}, f32[320,640]{1,0:T(8,128)}, u32[]{:S(2)}, u32[]{:S(2)}) collective-permute-start(f32[320,640]{1,0:T(8,128)S(1)} %turn.1.refs_2_), channel_id=1, source_target_pairs={{8,0},{9,1},{10,2},{11,3},{12,4},{13,5},{14,6},{15,7},{16,8},{17,9... | collective-permute-start | bytes 2457608 | tf_op jit(solution)/shard_map/send1/ppermute | solution.py:323
  10.1 11.0 %collective-permute-start.2 = (f32[160,640]{1,0:T(8,128)S(1)}, f32[160,640]{1,0:T(8,128)S(1)}, u32[]{:S(2)}, u32[]{:S(2)}) collective-permute-start(f32[160,640]{1,0:T(8,128)S(1)} %get-tuple-element.50), channel_id=1, source_target_pairs={{0,4},{1,5},{2,6},{3,7},{4,0},{5,1},{6,2},{7,3},{8,12},{9,13},{10,... | collective-permute-start | bytes 1228808 | tf_op jit(solution)/shard_map/send2/ppermute | solution.py:323
  19.4 21.2 %collective-permute-start.6 = (f32[4,8,6400]{2,1,0:T(8,128)S(1)}, f32[4,8,6400]{2,1,0:T(8,128)S(1)}, u32[]{:S(2)}, u32[]{:S(2)}) collective-permute-start(f32[4,8,6400]{2,1,0:T(8,128)S(1)} %sort.1.refs_0_), channel_id=1, source_target_pairs={{0,2},{1,3},{2,0},{3,1},{4,6},{5,7},{6,4},{7,5},{8,10},{9,11},{10,... | collective-permute-start | bytes 2457608 | tf_op jit(solution)/shard_map/send3/ppermute | solution.py:323
  28.9 11.8 %collective-permute-start.3 = (f32[320,640]{1,0:T(8,128)}, f32[320,640]{1,0:T(8,128)}, u32[]{:S(2)}, u32[]{:S(2)}) collective-permute-start(f32[320,640]{1,0:T(8,128)} %collective-permute-done.refs_3_), channel_id=1, source_target_pairs={{8,16},{9,17},{10,18},{11,19},{12,20},{13,21},{14,22},{15,23},{16,... | collective-permute-start | bytes 2457608 | tf_op jit(solution)/shard_map/send5/ppermute | solution.py:323
  30.4 22.5 %collective-permute-start.4 = (f32[320,640]{1,0:T(8,128)}, f32[320,640]{1,0:T(8,128)}, u32[]{:S(2)}, u32[]{:S(2)}) collective-permute-start(f32[320,640]{1,0:T(8,128)} %collective-permute-done.1.refs_4_), channel_id=1, source_target_pairs={{8,0},{9,1},{10,2},{11,3},{12,4},{13,5},{14,6},{15,7},{16,8},{17,9... | collective-permute-start | bytes 2457608 | tf_op jit(solution)/shard_map/send6/ppermute | solution.py:323
  31.7 24.8 %copy-start.9 = (s32[4,2]{0,1:T(2,128)S(1)}, s32[4,2]{0,1:T(2,128)}, u32[]{:S(2)}) copy-start(s32[4,2]{0,1:T(2,128)} %param.7) | copy-start | bytes 100
  32.0 21.0 %collective-permute-start.5 = (f32[320,640]{1,0:T(8,128)S(1)}, f32[320,640]{1,0:T(8,128)S(1)}, u32[]{:S(2)}, u32[]{:S(2)}) collective-permute-start(f32[320,640]{1,0:T(8,128)S(1)} %join.1.refs_0_), channel_id=1, source_target_pairs={{0,1},{1,0},{2,3},{3,2},{4,5},{5,4},{6,7},{7,6},{8,9},{9,8},{10,11... | collective-permute-start | bytes 2457608 | tf_op jit(solution)/shard_map/send8/ppermute | solution.py:323
  32.0 24.5 %collective-permute-start.7 = (f32[320,640]{1,0:T(8,128)S(1)}, f32[320,640]{1,0:T(8,128)}, u32[]{:S(2)}, u32[]{:S(2)}) collective-permute-start(f32[320,640]{1,0:T(8,128)S(1)} %join.1.refs_0_), channel_id=1, source_target_pairs={{0,2},{1,3},{2,0},{3,1},{4,6},{5,7},{6,4},{7,5},{8,10},{9,11},{10,... | collective-permute-start | bytes 2457608 | tf_op jit(solution)/shard_map/send7/ppermute | solution.py:323
  32.6 0.9 copy-start.3
  40.6 18.9 %collective-permute-start.10 = (f32[4,8,6400]{2,1,0:T(8,128)S(1)}, f32[4,8,6400]{2,1,0:T(8,128)S(1)}, u32[]{:S(2)}, u32[]{:S(2)}) collective-permute-start(f32[4,8,6400]{2,1,0:T(8,128)S(1)} %sort.1.refs_0_), channel_id=1, source_target_pairs={{0,1},{1,0},{2,3},{3,2},{4,5},{5,4},{6,7},{7,6},{8,9},{9,8},{10,11... | collective-permute-start | bytes 2457608 | tf_op jit(solution)/shard_map/send4/ppermute | solution.py:323
  52.9 0.9 copy-start.5
  53.8 5.7 %collective-permute-start.11 = (f32[4,8,6400]{2,1,0:T(8,128)S(1)}, f32[4,8,6400]{2,1,0:T(8,128)S(1)}, u32[]{:S(2)}, u32[]{:S(2)}) collective-permute-start(f32[4,8,6400]{2,1,0:T(8,128)S(1)} %collective-permute-done.6.refs_2_), channel_id=1, source_target_pairs={{0,1},{1,0},{2,3},{3,2},{4,5},{5,4},{6,7},{7,6},{8,9},{9,8},{10,11... | collective-permute-start | bytes 2457608 | tf_op jit(solution)/shard_map/send11/ppermute | solution.py:323
  56.5 9.5 %collective-permute-start.8 = (f32[320,640]{1,0:T(8,128)}, f32[320,640]{1,0:T(8,128)}, u32[]{:S(2)}, u32[]{:S(2)}) collective-permute-start(f32[320,640]{1,0:T(8,128)} %collective-permute-done.7.refs_2_), channel_id=1, source_target_pairs={{0,1},{1,0},{2,3},{3,2},{4,5},{5,4},{6,7},{7,6},{8,9},{9,8},{10,11... | collective-permute-start | bytes 2457608 | tf_op jit(solution)/shard_map/send10/ppermute | solution.py:323
  57.9 8.1 %copy-start.4 = (f32[320,640]{1,0:T(8,128)S(1)}, f32[320,640]{1,0:T(8,128)}, u32[]{:S(2)}) copy-start(f32[320,640]{1,0:T(8,128)} %copy-done.3) | copy-start | bytes 2457604
  57.9 8.1 %copy-start.6 = (f32[320,640]{1,0:T(8,128)S(1)}, f32[320,640]{1,0:T(8,128)}, u32[]{:S(2)}) copy-start(f32[320,640]{1,0:T(8,128)} %copy-done.5) | copy-start | bytes 2457604
  57.9 22.7 %collective-permute-start.9 = (f32[320,640]{1,0:T(8,128)S(1)}, f32[320,640]{1,0:T(8,128)S(1)}, u32[]{:S(2)}, u32[]{:S(2)}) collective-permute-start(f32[320,640]{1,0:T(8,128)S(1)} %broadcast_select_fusion.refs_5_), channel_id=1, source_target_pairs={{8,0},{9,1},{10,2},{11,3},{12,4},{13,5},{14,6},{15,7},{16,24},{17,... | collective-permute-start | bytes 2457608 | tf_op jit(solution)/shard_map/send9/ppermute | solution.py:323
  66.0 2.0 %copy-start.2 = (f32[320,640]{1,0:T(8,128)S(1)}, f32[320,640]{1,0:T(8,128)}, u32[]{:S(2)}) copy-start(f32[320,640]{1,0:T(8,128)} %copy-done.1) | copy-start | bytes 2457604
  82.2 11.4 %collective-permute-start.12 = (f32[160,640]{1,0:T(8,128)S(1)}, f32[160,640]{1,0:T(8,128)S(1)}, u32[]{:S(2)}, u32[]{:S(2)}) collective-permute-start(f32[160,640]{1,0:T(8,128)S(1)} %get-tuple-element.66), channel_id=1, source_target_pairs={{0,4},{1,5},{2,6},{3,7},{4,0},{5,1},{6,2},{7,3},{8,12},{9,13},{10,... | collective-permute-start | bytes 1228808 | tf_op jit(solution)/shard_map/send12/ppermute | solution.py:323
  93.6 15.7 %collective-permute-start.13 = (f32[160,640]{1,0:T(8,128)S(1)}, f32[160,640]{1,0:T(8,128)S(1)}, u32[]{:S(2)}, u32[]{:S(2)}) collective-permute-start(f32[160,640]{1,0:T(8,128)S(1)} %get-tuple-element.75), channel_id=1, source_target_pairs={{0,4},{1,5},{2,6},{3,7},{4,0},{5,1},{6,2},{7,3},{8,12},{9,13},{10,... | collective-permute-start | bytes 1228808 | tf_op jit(solution)/shard_map/send13/ppermute | solution.py:323
  96.1 0.8 copy-start.7
  96.9 25.1 %collective-permute-start.14 = (f32[80,640]{1,0:T(8,128)}, f32[80,640]{1,0:T(8,128)S(1)}, u32[]{:S(2)}, u32[]{:S(2)}) collective-permute-start(f32[80,640]{1,0:T(8,128)} %get-tuple-element.82), channel_id=1, source_target_pairs={{0,0},{1,8},{2,16},{3,24},{4,4},{5,12},{6,20},{7,28},{8,1},{9,9},{... | collective-permute-start | bytes 614408 | tf_op jit(solution)/shard_map/send14/ppermute | solution.py:323
  101.4 20.5 %collective-permute-start.15 = (f32[80,640]{1,0:T(8,128)}, f32[80,640]{1,0:T(8,128)}, u32[]{:S(2)}, u32[]{:S(2)}) collective-permute-start(f32[80,640]{1,0:T(8,128)} %get-tuple-element.83), channel_id=1, source_target_pairs={{0,4},{1,12},{2,20},{3,28},{4,0},{5,8},{6,16},{7,24},{8,5},{9,13},... | collective-permute-start | bytes 614408 | tf_op jit(solution)/shard_map/send15/ppermute | solution.py:323
  109.4 5.0 %collective-permute-start.20 = (f32[4,2,8,200]{3,2,1,0:T(8,128)S(1)}, f32[4,2,8,200]{3,2,1,0:T(8,128)S(1)}, u32[]{:S(2)}, u32[]{:S(2)}) collective-permute-start(f32[4,2,8,200]{3,2,1,0:T(8,128)S(1)} %get-tuple-element.92), channel_id=1, source_target_pairs={{0,3},{1,2},{2,1},{3,0},{4,7},{5,6},{6,5},{7,4},{8,11},{9,10},{10,... | collective-permute-start | bytes 153608 | tf_op jit(solution)/shard_map/send20/ppermute | solution.py:323
  109.5 8.6 %collective-permute-start.19 = (f32[4,2,8,200]{3,2,1,0:T(8,128)S(1)}, f32[4,2,8,200]{3,2,1,0:T(8,128)S(1)}, u32[]{:S(2)}, u32[]{:S(2)}) collective-permute-start(f32[4,2,8,200]{3,2,1,0:T(8,128)S(1)} %get-tuple-element.93), channel_id=1, source_target_pairs={{0,2},{1,3},{2,0},{3,1},{4,6},{5,7},{6,4},{7,5},{8,10},{9,11},{10,... | collective-permute-start | bytes 153608 | tf_op jit(solution)/shard_map/send19/ppermute | solution.py:323
  111.8 9.4 %collective-permute-start.18 = (f32[4,2,8,200]{3,2,1,0:T(8,128)S(1)}, f32[4,2,8,200]{3,2,1,0:T(8,128)S(1)}, u32[]{:S(2)}, u32[]{:S(2)}) collective-permute-start(f32[4,2,8,200]{3,2,1,0:T(8,128)S(1)} %get-tuple-element.94), channel_id=1, source_target_pairs={{0,1},{1,0},{2,3},{3,2},{4,5},{5,4},{6,7},{7,6},{8,9},{9,8},{10,11... | collective-permute-start | bytes 153608 | tf_op jit(solution)/shard_map/send18/ppermute | solution.py:323
  114.4 20.2 %collective-permute-start.16 = (f32[80,640]{1,0:T(8,128)S(1)}, f32[80,640]{1,0:T(8,128)S(1)}, u32[]{:S(2)}, u32[]{:S(2)}) collective-permute-start(f32[80,640]{1,0:T(8,128)S(1)} %get-tuple-element.84), channel_id=1, source_target_pairs={{0,0},{1,8},{2,16},{3,24},{4,4},{5,12},{6,20},{7,28},{8,1},{9,9},{... | collective-permute-start | bytes 614408 | tf_op jit(solution)/shard_map/send16/ppermute | solution.py:323
  118.0 18.8 %collective-permute-start.17 = (f32[80,640]{1,0:T(8,128)S(1)}, f32[80,640]{1,0:T(8,128)S(1)}, u32[]{:S(2)}, u32[]{:S(2)}) collective-permute-start(f32[80,640]{1,0:T(8,128)S(1)} %get-tuple-element.85), channel_id=1, source_target_pairs={{0,4},{1,12},{2,20},{3,28},{4,0},{5,8},{6,16},{7,24},{8,5},{9,13},... | collective-permute-start | bytes 614408 | tf_op jit(solution)/shard_map/send17/ppermute | solution.py:323
  121.2 15.7 %copy-start.8 = (f32[160,640]{1,0:T(8,128)S(1)}, f32[160,640]{1,0:T(8,128)}, u32[]{:S(2)}) copy-start(f32[160,640]{1,0:T(8,128)} %copy-done.7) | copy-start | bytes 1228804

commit v3 on v2

--- a/solution.py
+++ b/solution.py
@@ -360,13 +360,13 @@
     (kinds,) = whole(
         sort_kernel, "sort", 30, [(NIRR, rows_i * cols_j, flat // NIRR)], (amplitudes,)
     )
-    kinds_x, kinds_k = swap_x(kinds), swap(kinds)
-    a1, b1, got, kinds = after((a1, b1, got, kinds))
-
-    a2, b2 = up(a1, (1, 2)), down(b1, (1, 2))
     (u,) = whole(join_kernel, "join", 1, [(rows_i * v, cols_j * v)], (keep, got))
     u_x, u_k = swap_x(u), swap(u)
-    a2, b2, u_k, kinds_x = after((a2, b2, u_k, kinds_x))
+    a1, b1, u, kinds = after((a1, b1, u, kinds))
+
+    a2, b2 = up(a1, (1, 2)), down(b1, (1, 2))
+    kinds_x, kinds_k = swap_x(kinds), swap(kinds)
+    a2, b2, u_k, kinds_k = after((a2, b2, u_k, kinds_k))
 
     c2 = jnp.where(lax.axis_index("row") < 4, b2, a2)
     c3 = ends(c2)

time: 142 us -> 139 us (0.979)
  waiting for transfers between devices: 54.2 us -> 51.9 us
  local copies, waits for them, and re-layouts: 7.98 us -> 9.43 us
    ppermute x21, waiting for transfers between devices: 54.2 us -> 51.9 us  [send(): return lax.ppermute(a, AXES, permutation(rule))]
    unnamed x23, local copies, waits for them, and re-layouts: 2.67 us -> 4.12 us
  transfers between devices with their start and end apart: 21 -> 21, of which waited for: 11 -> 9; matrix products, arithmetic and copies ran while one was open for 2% -> 2% of each run, Pallas kernels for 30% -> 30%
where the time goes in v3:
time: 139 us
  waiting for transfers between devices  51.9 us (37%)
  Pallas kernels  46.4 us (33%)
  starting transfers between devices  29.5 us (21%)
  local copies, waits for them, and re-layouts  9.43 us (7%)
    ppermute x21, waiting for transfers between devices, send(): return lax.ppermute(a, AXES, permutation(rule))  51.9 us
    ppermute x21, starting transfers between devices, send(): return lax.ppermute(a, AXES, permutation(rule))  29.5 us
    pallas_call x3, Pallas kernels, ladder_part(): pl.pallas_call(ladder_kernel, out_shape=jax.ShapeDtypeStruct((count, pair...  23.8 us
    pallas_call x10, Pallas kernels, whole(): pl.pallas_call(kernel, out_shape=[jax.ShapeDtypeStruct(shape, dtype) for...  22.6 us
    unnamed x23, local copies, waits for them, and re-layouts  4.12 us
  transfers between devices with their start and end apart: 21, of which 9 were waited for; matrix products, arithmetic and copies ran while one was open for 2% of the time, Pallas kernels for 30%

profile of v3, /device:TPU:2, one launch (start us, length us, event | category | flops | bytes accessed | tf_op | source)
XLA Modules:
  0.0 138.8 jit_solution(12626117379143598271)
XLA Ops:
  0.0 2.0 %reshape.12.four_ref = f32[2,4,160,160]{3,2,1,0:T(8,128)S(1)} reshape(f32[2,4,25600]{2,1,0:T(4,128)} %param.5) | data formatting | bytes 1638400 | tf_op jit(solution)/shard_map/reshape | solution.py:354
  2.0 0.0 copy-start
  2.0 0.8 turn.1.refs_2_
  2.8 0.4 copy-done
  3.1 0.8 reshape.13.four_ref
  3.9 0.8 pair.1
  4.7 1.6 %collective-permute-start.2 = (f32[160,640]{1,0:T(8,128)S(1)}, f32[160,640]{1,0:T(8,128)S(1)}, u32[]{:S(2)}, u32[]{:S(2)}) collective-permute-start(f32[160,640]{1,0:T(8,128)S(1)} %get-tuple-element.50), channel_id=1, source_target_pairs={{0,4},{1,5},{2,6},{3,7},{4,0},{5,1},{6,2},{7,3},{8,12},{9,13},{10,... | collective-permute-start | bytes 1228808 | tf_op jit(solution)/shard_map/send2/ppermute | solution.py:323
  6.3 4.4 %collective-permute-start = (f32[320,640]{1,0:T(8,128)S(1)}, f32[320,640]{1,0:T(8,128)}, u32[]{:S(2)}, u32[]{:S(2)}) collective-permute-start(f32[320,640]{1,0:T(8,128)S(1)} %turn.1.refs_2_), channel_id=1, source_target_pairs={{0,8},{1,9},{2,10},{3,11},{4,12},{5,13},{6,14},{7,15},{8,16},{9,17... | collective-permute-start | bytes 2457608 | tf_op jit(solution)/shard_map/send0/ppermute | solution.py:323
  10.7 1.3 collective-permute-start.1
  12.0 4.0 %collective-permute-done.2.got_ref = f32[160,640]{1,0:T(8,128)S(1)} collective-permute-done((f32[160,640]{1,0:T(8,128)S(1)}, f32[160,640]{1,0:T(8,128)S(1)}, u32[]{:S(2)}, u32[]{:S(2)}) %collective-permute-start.2) | collective-permute-done | bytes 409632 | tf_op jit(solution)/shard_map/send2/ppermute | solution.py:323
  16.0 0.2 join.1.refs_0_
  16.2 0.0 copy-start.1
  16.2 0.0 copy-start.9
  16.2 0.1 collective-permute-start.5
  16.3 0.4 collective-permute-start.7
  16.7 7.7 %sort.1.refs_0_ = f32[4,8,6400]{2,1,0:T(8,128)S(1)} custom-call(f32[2,4,25600]{2,1,0:T(4,128)S(1)} %copy-done), custom_call_target="tpu_custom_call" | custom-call | flops 30000001024 | bytes 90000000 | tf_op jit(solution)/shard_map/sort/pallas_call | solution.py:143
  24.4 2.6 %collective-permute-done.refs_3_ = f32[320,640]{1,0:T(8,128)} collective-permute-done((f32[320,640]{1,0:T(8,128)S(1)}, f32[320,640]{1,0:T(8,128)}, u32[]{:S(2)}, u32[]{:S(2)}) %collective-permute-start) | collective-permute-done | bytes 819232 | tf_op jit(solution)/shard_map/send0/ppermute | solution.py:323
  27.0 5.1 %collective-permute-done.1.refs_4_ = f32[320,640]{1,0:T(8,128)} collective-permute-done((f32[320,640]{1,0:T(8,128)S(1)}, f32[320,640]{1,0:T(8,128)}, u32[]{:S(2)}, u32[]{:S(2)}) %collective-permute-start.1) | collective-permute-done | bytes 819232 | tf_op jit(solution)/shard_map/send1/ppermute | solution.py:323
  32.1 1.6 %collective-permute-start.3 = (f32[320,640]{1,0:T(8,128)}, f32[320,640]{1,0:T(8,128)}, u32[]{:S(2)}, u32[]{:S(2)}) collective-permute-start(f32[320,640]{1,0:T(8,128)} %collective-permute-done.refs_3_), channel_id=1, source_target_pairs={{8,16},{9,17},{10,18},{11,19},{12,20},{13,21},{14,22},{15,23},{16,... | collective-permute-start | bytes 2457608 | tf_op jit(solution)/shard_map/send5/ppermute | solution.py:323
  33.7 1.3 collective-permute-start.4
  35.0 0.1 collective-permute-start.6
  35.0 0.0 collective-permute-done.5.refs_1_
  35.1 0.9 copy-done.3
  35.9 0.5 collective-permute-start.10
  36.5 0.6 collective-permute-done.7.refs_2_
  37.1 0.0 collective-permute-start.8
  37.1 0.1 copy.9.info.window
  37.2 0.0 collective-permute-done.3
  37.2 18.7 %collective-permute-done.4 = f32[320,640]{1,0:T(8,128)} collective-permute-done((f32[320,640]{1,0:T(8,128)}, f32[320,640]{1,0:T(8,128)}, u32[]{:S(2)}, u32[]{:S(2)}) %collective-permute-start.4) | collective-permute-done | bytes 819232 | tf_op jit(solution)/shard_map/send6/ppermute | solution.py:323
  55.9 0.0 collective-permute-done.6.refs_1_
  55.9 1.2 broadcast_select_fusion.refs_5_
  57.1 1.5 %collective-permute-start.9 = (f32[320,640]{1,0:T(8,128)S(1)}, f32[320,640]{1,0:T(8,128)S(1)}, u32[]{:S(2)}, u32[]{:S(2)}) collective-permute-start(f32[320,640]{1,0:T(8,128)S(1)} %broadcast_select_fusion.refs_5_), channel_id=1, source_target_pairs={{8,0},{9,1},{10,2},{11,3},{12,4},{13,5},{14,6},{15,7},{16,24},{17,... | collective-permute-start | bytes 2457608 | tf_op jit(solution)/shard_map/send9/ppermute | solution.py:323
  58.6 0.1 collective-permute-start.11
  58.7 0.0 collective-permute-done.8.refs_3_
  58.7 1.9 %arrange.1 = (bf16[4,320,640]{2,1,0:T(8,128)(2,1)S(1)}, bf16[4,320,640]{2,1,0:T(8,128)(2,1)S(1)}) custom-call(f32[320,640]{1,0:T(8,128)S(1)} %copy-done.2, f32[320,640]{1,0:T(8,128)S(1)} %copy-done.4, f32[320,640]{1,0:T(8,128)} %collective-permute-done.7.refs_2_, f32[320,640]{1,0:T(8,128)} %collective-permute-done.8.refs_3_), custom_call_target="tpu_custom_call" | custom-call | flops 3000000000 | bytes 9000000 | tf_op jit(solution)/shard_map/arrange/pallas_call | solution.py:143
  60.6 7.2 %cycle.2.refs_2_ = f32[640,640]{1,0:T(8,128)S(1)} custom-call(bf16[4,320,640]{2,1,0:T(8,128)(2,1)S(1)} %get-tuple-element.57.refs_0_, bf16[4,320,640]{2,1,0:T(8,128)(2,1)S(1)} %get-tuple-element.58.refs_1_, f32[320,640]{1,0:T(8,128)S(1)} %turn.1.refs_2_, f32[320,640]{1,0:T(8,128)} %collective-permute-done.refs_3_, ...), custom_call_target="tpu_custom_call" | custom-call | flops 5800000000 | bytes 17400000 | tf_op jit(solution)/shard_map/cycle/pallas_call | solution.py:143
  67.8 0.0 collective-permute-done.11.refs_3_
  67.8 6.5 %ladder.3 = f32[1,2,32,200]{3,2,1,0:T(8,128)S(1)} custom-call(s32[4,2]{1,0:T(4,128)S(1)} %copy.9.info.window, f32[4,8,6400]{2,1,0:T(8,128)S(1)} %sort.1.refs_0_, f32[4,8,6400]{2,1,0:T(8,128)S(1)} %collective-permute-done.6.refs_1_, f32[4,8,6400]{2,1,0:T(8,128)S(1)} %collective-permute-done.10.refs_2_, f32[4,8,6400]{2,1,0:T(8,128)S(1)} %collective-permute-done.11.refs_3_, ...), custom_call_target="tpu_custom_call" | custom-call | flops 5500000256 | bytes 16500000 | tf_op jit(solution)/shard_map/ladder/pallas_call | solution.py:118
  74.3 2.3 %collective-permute-done.9.refs_3_ = f32[320,640]{1,0:T(8,128)S(1)} collective-permute-done((f32[320,640]{1,0:T(8,128)S(1)}, f32[320,640]{1,0:T(8,128)S(1)}, u32[]{:S(2)}, u32[]{:S(2)}) %collective-permute-start.9) | collective-permute-done | bytes 819232 | tf_op jit(solution)/shard_map/send9/ppermute | solution.py:323
  76.6 1.7 %cycle.3 = (f32[160,640]{1,0:T(8,128)S(1)}, f32[160,640]{1,0:T(8,128)S(1)}, f32[160,640]{1,0:T(8,128)S(1)}, f32[160,640]{1,0:T(8,128)S(1)}) custom-call(bf16[4,320,640]{2,1,0:T(8,128)(2,1)S(1)} %get-tuple-element.57.refs_0_, bf16[4,320,640]{2,1,0:T(8,128)(2,1)S(1)} %get-tuple-element.58.refs_1_, f32[640,640]{1,0:T(8,128)S(1)} %cycle.2.refs_2_, ...), custom_call_target="tpu_custom_call" | custom-call | flops 2200000000 | bytes 6600000 | tf_op jit(solution)/shard_map/cycle/pallas_call | solution.py:143
  78.3 0.6 collective-permute-start.12
  78.8 10.8 %ladder.4 = f32[2,2,32,200]{3,2,1,0:T(8,128)S(1)} custom-call(s32[4,2]{1,0:T(4,128)S(1)} %copy.9.info.window, f32[4,8,6400]{2,1,0:T(8,128)S(1)} %sort.1.refs_0_, f32[4,8,6400]{2,1,0:T(8,128)S(1)} %collective-permute-done.6.refs_1_, f32[4,8,6400]{2,1,0:T(8,128)S(1)} %collective-permute-done.10.refs_2_, f32[4,8,6400]{2,1,0:T(8,128)S(1)} %collective-permute-done.11.refs_3_, ...), custom_call_target="tpu_custom_call" | custom-call | flops 11000000512 | bytes 33000000 | tf_op jit(solution)/shard_map/ladder/pallas_call | solution.py:118
  89.6 1.6 %collective-permute-start.13 = (f32[160,640]{1,0:T(8,128)S(1)}, f32[160,640]{1,0:T(8,128)S(1)}, u32[]{:S(2)}, u32[]{:S(2)}) collective-permute-start(f32[160,640]{1,0:T(8,128)S(1)} %get-tuple-element.75), channel_id=1, source_target_pairs={{0,4},{1,5},{2,6},{3,7},{4,0},{5,1},{6,2},{7,3},{8,12},{9,13},{10,... | collective-permute-start | bytes 1228808 | tf_op jit(solution)/shard_map/send13/ppermute | solution.py:323
  91.2 0.1 add.8
  91.4 0.0 copy-start.5
  91.4 0.7 copy-done.5
  92.1 4.1 %collective-permute-start.14 = (f32[80,640]{1,0:T(8,128)S(1)}, f32[80,640]{1,0:T(8,128)S(1)}, u32[]{:S(2)}, u32[]{:S(2)}) collective-permute-start(f32[80,640]{1,0:T(8,128)S(1)} %get-tuple-element.82), channel_id=1, source_target_pairs={{0,0},{1,8},{2,16},{3,24},{4,4},{5,12},{6,20},{7,28},{8,1},{9,9},{... | collective-permute-start | bytes 614408 | tf_op jit(solution)/shard_map/send14/ppermute | solution.py:323
  96.2 1.8 %collective-permute-start.15 = (f32[80,640]{1,0:T(8,128)S(1)}, f32[80,640]{1,0:T(8,128)S(1)}, u32[]{:S(2)}, u32[]{:S(2)}) collective-permute-start(f32[80,640]{1,0:T(8,128)S(1)} %get-tuple-element.83), channel_id=1, source_target_pairs={{0,4},{1,12},{2,20},{3,28},{4,0},{5,8},{6,16},{7,24},{8,5},{9,13},... | collective-permute-start | bytes 614408 | tf_op jit(solution)/shard_map/send15/ppermute | solution.py:323
  98.1 6.5 %ladder.5 = f32[1,2,32,200]{3,2,1,0:T(8,128)S(1)} custom-call(s32[4,2]{1,0:T(4,128)S(1)} %copy.9.info.window, f32[4,8,6400]{2,1,0:T(8,128)S(1)} %sort.1.refs_0_, f32[4,8,6400]{2,1,0:T(8,128)S(1)} %collective-permute-done.6.refs_1_, f32[4,8,6400]{2,1,0:T(8,128)S(1)} %collective-permute-done.10.refs_2_, f32[4,8,6400]{2,1,0:T(8,128)S(1)} %collective-permute-done.11.refs_3_, ...), custom_call_target="tpu_custom_call" | custom-call | flops 5500000256 | bytes 16500000 | tf_op jit(solution)/shard_map/ladder/pallas_call | solution.py:118
  104.6 0.1 collective-permute-start.20
  104.7 0.1 collective-permute-start.19
  104.8 1.8 %collective-permute-start.18 = (f32[4,2,8,200]{3,2,1,0:T(8,128)S(1)}, f32[4,2,8,200]{3,2,1,0:T(8,128)S(1)}, u32[]{:S(2)}, u32[]{:S(2)}) collective-permute-start(f32[4,2,8,200]{3,2,1,0:T(8,128)S(1)} %get-tuple-element.94), channel_id=1, source_target_pairs={{0,1},{1,0},{2,3},{3,2},{4,5},{5,4},{6,7},{7,6},{8,9},{9,8},{10,11... | collective-permute-start | bytes 153608 | tf_op jit(solution)/shard_map/send18/ppermute | solution.py:323
  106.6 0.1 add.9
  106.7 3.1 %collective-permute-done.20 = f32[4,2,8,200]{3,2,1,0:T(8,128)S(1)} collective-permute-done((f32[4,2,8,200]{3,2,1,0:T(8,128)S(1)}, f32[4,2,8,200]{3,2,1,0:T(8,128)S(1)}, u32[]{:S(2)}, u32[]{:S(2)}) %collective-permute-start.20) | collective-permute-done | bytes 51232 | tf_op jit(solution)/shard_map/send20/ppermute | solution.py:323
  109.8 4.4 %collective-permute-start.16 = (f32[80,640]{1,0:T(8,128)S(1)}, f32[80,640]{1,0:T(8,128)S(1)}, u32[]{:S(2)}, u32[]{:S(2)}) collective-permute-start(f32[80,640]{1,0:T(8,128)S(1)} %get-tuple-element.84), channel_id=1, source_target_pairs={{0,0},{1,8},{2,16},{3,24},{4,4},{5,12},{6,20},{7,28},{8,1},{9,9},{... | collective-permute-start | bytes 614408 | tf_op jit(solution)/shard_map/send16/ppermute | solution.py:323
  114.2 2.4 %collective-permute-start.17 = (f32[80,640]{1,0:T(8,128)S(1)}, f32[80,640]{1,0:T(8,128)S(1)}, u32[]{:S(2)}, u32[]{:S(2)}) collective-permute-start(f32[80,640]{1,0:T(8,128)S(1)} %get-tuple-element.85), channel_id=1, source_target_pairs={{0,4},{1,12},{2,20},{3,28},{4,0},{5,8},{6,16},{7,24},{8,5},{9,13},... | collective-permute-start | bytes 614408 | tf_op jit(solution)/shard_map/send17/ppermute | solution.py:323
  116.7 0.1 copy.8
  116.8 0.5 reshape.14.ladder_ref
  117.4 11.0 %collective-permute-done.16.s1_ref = f32[80,640]{1,0:T(8,128)S(1)} collective-permute-done((f32[80,640]{1,0:T(8,128)S(1)}, f32[80,640]{1,0:T(8,128)S(1)}, u32[]{:S(2)}, u32[]{:S(2)}) %collective-permute-start.16) | collective-permute-done | bytes 204832 | tf_op jit(solution)/shard_map/send16/ppermute | solution.py:323
  128.3 4.4 %collective-permute-done.17.c1_ref = f32[80,640]{1,0:T(8,128)S(1)} collective-permute-done((f32[80,640]{1,0:T(8,128)S(1)}, f32[80,640]{1,0:T(8,128)S(1)}, u32[]{:S(2)}, u32[]{:S(2)}) %collective-permute-start.17) | collective-permute-done | bytes 204832 | tf_op jit(solution)/shard_map/send17/ppermute | solution.py:323
  132.8 1.0 copy-done.6
  133.8 1.0 copy-done.8
  134.8 2.2 %merge.1 = f32[2,4,160,160]{3,2,1,0:T(8,128)S(1)} custom-call(s32[4,2]{1,0:T(4,128)S(1)} %copy.9.info.window, f32[160,640]{1,0:T(8,128)S(1)} %copy-done.6, f32[160,640]{1,0:T(8,128)S(1)} %copy-done.8, f32[80,640]{1,0:T(8,128)S(1)} %collective-permute-done.14.s0_ref, f32[80,640]{1,0:T(8,128)S(1)} %collective-permute-done.15.c0_ref, ...), custom_call_target="tpu_custom_call" | custom-call | flops 2000000000 | bytes 6000000 | tf_op jit(solution)/shard_map/merge/pallas_call | solution.py:143
  137.0 1.9 %reshape.15 = f32[2,4,25600]{2,1,0:T(4,128)} reshape(f32[2,4,160,160]{3,2,1,0:T(8,128)S(1)} %merge.1) | data formatting | bytes 1638400 | tf_op jit(solution)/shard_map/reshape | solution.py:409
  (25 shorter events, 0.2 us)
Async XLA Ops:
  2.0 1.2 copy-start
  4.7 11.3 %collective-permute-start.2 = (f32[160,640]{1,0:T(8,128)S(1)}, f32[160,640]{1,0:T(8,128)S(1)}, u32[]{:S(2)}, u32[]{:S(2)}) collective-permute-start(f32[160,640]{1,0:T(8,128)S(1)} %get-tuple-element.50), channel_id=1, source_target_pairs={{0,4},{1,5},{2,6},{3,7},{4,0},{5,1},{6,2},{7,3},{8,12},{9,13},{10,... | collective-permute-start | bytes 1228808 | tf_op jit(solution)/shard_map/send2/ppermute | solution.py:323
  6.3 20.7 %collective-permute-start = (f32[320,640]{1,0:T(8,128)S(1)}, f32[320,640]{1,0:T(8,128)}, u32[]{:S(2)}, u32[]{:S(2)}) collective-permute-start(f32[320,640]{1,0:T(8,128)S(1)} %turn.1.refs_2_), channel_id=1, source_target_pairs={{0,8},{1,9},{2,10},{3,11},{4,12},{5,13},{6,14},{7,15},{8,16},{9,17... | collective-permute-start | bytes 2457608 | tf_op jit(solution)/shard_map/send0/ppermute | solution.py:323
  10.7 21.4 %collective-permute-start.1 = (f32[320,640]{1,0:T(8,128)S(1)}, f32[320,640]{1,0:T(8,128)}, u32[]{:S(2)}, u32[]{:S(2)}) collective-permute-start(f32[320,640]{1,0:T(8,128)S(1)} %turn.1.refs_2_), channel_id=1, source_target_pairs={{8,0},{9,1},{10,2},{11,3},{12,4},{13,5},{14,6},{15,7},{16,8},{17,9... | collective-permute-start | bytes 2457608 | tf_op jit(solution)/shard_map/send1/ppermute | solution.py:323
  16.2 8.2 %copy-start.1 = (f32[320,640]{1,0:T(8,128)}, f32[320,640]{1,0:T(8,128)S(1)}, u32[]{:S(2)}) copy-start(f32[320,640]{1,0:T(8,128)S(1)} %join.1.refs_0_) | copy-start | bytes 2457604
  16.2 20.9 %copy-start.9 = (s32[4,2]{0,1:T(2,128)S(1)}, s32[4,2]{0,1:T(2,128)}, u32[]{:S(2)}) copy-start(s32[4,2]{0,1:T(2,128)} %param.7) | copy-start | bytes 100
  16.2 18.8 %collective-permute-start.5 = (f32[320,640]{1,0:T(8,128)S(1)}, f32[320,640]{1,0:T(8,128)S(1)}, u32[]{:S(2)}, u32[]{:S(2)}) collective-permute-start(f32[320,640]{1,0:T(8,128)S(1)} %join.1.refs_0_), channel_id=1, source_target_pairs={{0,1},{1,0},{2,3},{3,2},{4,5},{5,4},{6,7},{7,6},{8,9},{9,8},{10,11... | collective-permute-start | bytes 2457608 | tf_op jit(solution)/shard_map/send4/ppermute | solution.py:323
  16.3 20.8 %collective-permute-start.7 = (f32[320,640]{1,0:T(8,128)S(1)}, f32[320,640]{1,0:T(8,128)}, u32[]{:S(2)}, u32[]{:S(2)}) collective-permute-start(f32[320,640]{1,0:T(8,128)S(1)} %join.1.refs_0_), channel_id=1, source_target_pairs={{0,2},{1,3},{2,0},{3,1},{4,6},{5,7},{6,4},{7,5},{8,10},{9,11},{10,... | collective-permute-start | bytes 2457608 | tf_op jit(solution)/shard_map/send3/ppermute | solution.py:323
  32.1 5.1 %collective-permute-start.3 = (f32[320,640]{1,0:T(8,128)}, f32[320,640]{1,0:T(8,128)}, u32[]{:S(2)}, u32[]{:S(2)}) collective-permute-start(f32[320,640]{1,0:T(8,128)} %collective-permute-done.refs_3_), channel_id=1, source_target_pairs={{8,16},{9,17},{10,18},{11,19},{12,20},{13,21},{14,22},{15,23},{16,... | collective-permute-start | bytes 2457608 | tf_op jit(solution)/shard_map/send5/ppermute | solution.py:323
  33.7 22.2 %collective-permute-start.4 = (f32[320,640]{1,0:T(8,128)}, f32[320,640]{1,0:T(8,128)}, u32[]{:S(2)}, u32[]{:S(2)}) collective-permute-start(f32[320,640]{1,0:T(8,128)} %collective-permute-done.1.refs_4_), channel_id=1, source_target_pairs={{8,0},{9,1},{10,2},{11,3},{12,4},{13,5},{14,6},{15,7},{16,8},{17,9... | collective-permute-start | bytes 2457608 | tf_op jit(solution)/shard_map/send6/ppermute | solution.py:323
  35.0 20.9 %collective-permute-start.6 = (f32[4,8,6400]{2,1,0:T(8,128)S(1)}, f32[4,8,6400]{2,1,0:T(8,128)S(1)}, u32[]{:S(2)}, u32[]{:S(2)}) collective-permute-start(f32[4,8,6400]{2,1,0:T(8,128)S(1)} %sort.1.refs_0_), channel_id=1, source_target_pairs={{0,1},{1,0},{2,3},{3,2},{4,5},{5,4},{6,7},{7,6},{8,9},{9,8},{10,11... | collective-permute-start | bytes 2457608 | tf_op jit(solution)/shard_map/send8/ppermute | solution.py:323
  35.1 0.9 copy-start.3
  35.9 22.7 %collective-permute-start.10 = (f32[4,8,6400]{2,1,0:T(8,128)S(1)}, f32[4,8,6400]{2,1,0:T(8,128)S(1)}, u32[]{:S(2)}, u32[]{:S(2)}) collective-permute-start(f32[4,8,6400]{2,1,0:T(8,128)S(1)} %sort.1.refs_0_), channel_id=1, source_target_pairs={{0,2},{1,3},{2,0},{3,1},{4,6},{5,7},{6,4},{7,5},{8,10},{9,11},{10,... | collective-permute-start | bytes 2457608 | tf_op jit(solution)/shard_map/send7/ppermute | solution.py:323
  37.1 21.6 %collective-permute-start.8 = (f32[320,640]{1,0:T(8,128)}, f32[320,640]{1,0:T(8,128)}, u32[]{:S(2)}, u32[]{:S(2)}) collective-permute-start(f32[320,640]{1,0:T(8,128)} %collective-permute-done.7.refs_2_), channel_id=1, source_target_pairs={{0,1},{1,0},{2,3},{3,2},{4,5},{5,4},{6,7},{7,6},{8,9},{9,8},{10,11... | collective-permute-start | bytes 2457608 | tf_op jit(solution)/shard_map/send10/ppermute | solution.py:323
  37.2 21.5 %copy-start.2 = (f32[320,640]{1,0:T(8,128)S(1)}, f32[320,640]{1,0:T(8,128)}, u32[]{:S(2)}) copy-start(f32[320,640]{1,0:T(8,128)} %copy-done.1) | copy-start | bytes 2457604
  37.2 21.5 %copy-start.4 = (f32[320,640]{1,0:T(8,128)S(1)}, f32[320,640]{1,0:T(8,128)}, u32[]{:S(2)}) copy-start(f32[320,640]{1,0:T(8,128)} %copy-done.3) | copy-start | bytes 2457604
  57.1 19.5 %collective-permute-start.9 = (f32[320,640]{1,0:T(8,128)S(1)}, f32[320,640]{1,0:T(8,128)S(1)}, u32[]{:S(2)}, u32[]{:S(2)}) collective-permute-start(f32[320,640]{1,0:T(8,128)S(1)} %broadcast_select_fusion.refs_5_), channel_id=1, source_target_pairs={{8,0},{9,1},{10,2},{11,3},{12,4},{13,5},{14,6},{15,7},{16,24},{17,... | collective-permute-start | bytes 2457608 | tf_op jit(solution)/shard_map/send9/ppermute | solution.py:323
  58.6 9.2 %collective-permute-start.11 = (f32[4,8,6400]{2,1,0:T(8,128)S(1)}, f32[4,8,6400]{2,1,0:T(8,128)S(1)}, u32[]{:S(2)}, u32[]{:S(2)}) collective-permute-start(f32[4,8,6400]{2,1,0:T(8,128)S(1)} %collective-permute-done.10.refs_2_), channel_id=1, source_target_pairs={{0,1},{1,0},{2,3},{3,2},{4,5},{5,4},{6,7},{7,6},{8,9},{9,8},{10,11... | collective-permute-start | bytes 2457608 | tf_op jit(solution)/shard_map/send11/ppermute | solution.py:323
  78.3 11.4 %collective-permute-start.12 = (f32[160,640]{1,0:T(8,128)S(1)}, f32[160,640]{1,0:T(8,128)S(1)}, u32[]{:S(2)}, u32[]{:S(2)}) collective-permute-start(f32[160,640]{1,0:T(8,128)S(1)} %get-tuple-element.66), channel_id=1, source_target_pairs={{0,4},{1,5},{2,6},{3,7},{4,0},{5,1},{6,2},{7,3},{8,12},{9,13},{10,... | collective-permute-start | bytes 1228808 | tf_op jit(solution)/shard_map/send12/ppermute | solution.py:323
  89.6 14.9 %collective-permute-start.13 = (f32[160,640]{1,0:T(8,128)S(1)}, f32[160,640]{1,0:T(8,128)S(1)}, u32[]{:S(2)}, u32[]{:S(2)}) collective-permute-start(f32[160,640]{1,0:T(8,128)S(1)} %get-tuple-element.75), channel_id=1, source_target_pairs={{0,4},{1,5},{2,6},{3,7},{4,0},{5,1},{6,2},{7,3},{8,12},{9,13},{10,... | collective-permute-start | bytes 1228808 | tf_op jit(solution)/shard_map/send13/ppermute | solution.py:323
  91.4 0.8 copy-start.5
  92.1 25.2 %collective-permute-start.14 = (f32[80,640]{1,0:T(8,128)S(1)}, f32[80,640]{1,0:T(8,128)S(1)}, u32[]{:S(2)}, u32[]{:S(2)}) collective-permute-start(f32[80,640]{1,0:T(8,128)S(1)} %get-tuple-element.82), channel_id=1, source_target_pairs={{0,0},{1,8},{2,16},{3,24},{4,4},{5,12},{6,20},{7,28},{8,1},{9,9},{... | collective-permute-start | bytes 614408 | tf_op jit(solution)/shard_map/send14/ppermute | solution.py:323
  96.2 21.1 %collective-permute-start.15 = (f32[80,640]{1,0:T(8,128)S(1)}, f32[80,640]{1,0:T(8,128)S(1)}, u32[]{:S(2)}, u32[]{:S(2)}) collective-permute-start(f32[80,640]{1,0:T(8,128)S(1)} %get-tuple-element.83), channel_id=1, source_target_pairs={{0,4},{1,12},{2,20},{3,28},{4,0},{5,8},{6,16},{7,24},{8,5},{9,13},... | collective-permute-start | bytes 614408 | tf_op jit(solution)/shard_map/send15/ppermute | solution.py:323
  104.6 5.2 %collective-permute-start.20 = (f32[4,2,8,200]{3,2,1,0:T(8,128)S(1)}, f32[4,2,8,200]{3,2,1,0:T(8,128)S(1)}, u32[]{:S(2)}, u32[]{:S(2)}) collective-permute-start(f32[4,2,8,200]{3,2,1,0:T(8,128)S(1)} %get-tuple-element.92), channel_id=1, source_target_pairs={{0,3},{1,2},{2,1},{3,0},{4,7},{5,6},{6,5},{7,4},{8,11},{9,10},{10,... | collective-permute-start | bytes 153608 | tf_op jit(solution)/shard_map/send20/ppermute | solution.py:323
  104.7 9.5 %collective-permute-start.19 = (f32[4,2,8,200]{3,2,1,0:T(8,128)S(1)}, f32[4,2,8,200]{3,2,1,0:T(8,128)S(1)}, u32[]{:S(2)}, u32[]{:S(2)}) collective-permute-start(f32[4,2,8,200]{3,2,1,0:T(8,128)S(1)} %get-tuple-element.93), channel_id=1, source_target_pairs={{0,2},{1,3},{2,0},{3,1},{4,6},{5,7},{6,4},{7,5},{8,10},{9,11},{10,... | collective-permute-start | bytes 153608 | tf_op jit(solution)/shard_map/send19/ppermute | solution.py:323
  104.8 11.8 %collective-permute-start.18 = (f32[4,2,8,200]{3,2,1,0:T(8,128)S(1)}, f32[4,2,8,200]{3,2,1,0:T(8,128)S(1)}, u32[]{:S(2)}, u32[]{:S(2)}) collective-permute-start(f32[4,2,8,200]{3,2,1,0:T(8,128)S(1)} %get-tuple-element.94), channel_id=1, source_target_pairs={{0,1},{1,0},{2,3},{3,2},{4,5},{5,4},{6,7},{7,6},{8,9},{9,8},{10,11... | collective-permute-start | bytes 153608 | tf_op jit(solution)/shard_map/send18/ppermute | solution.py:323
  106.7 10.6 %copy-start.7 = (f32[160,640]{1,0:T(8,128)}, f32[160,640]{1,0:T(8,128)S(1)}, u32[]{:S(2)}) copy-start(f32[160,640]{1,0:T(8,128)S(1)} %get-tuple-element.81.one_ref) | copy-start | bytes 1228804
  109.8 18.5 %collective-permute-start.16 = (f32[80,640]{1,0:T(8,128)S(1)}, f32[80,640]{1,0:T(8,128)S(1)}, u32[]{:S(2)}, u32[]{:S(2)}) collective-permute-start(f32[80,640]{1,0:T(8,128)S(1)} %get-tuple-element.84), channel_id=1, source_target_pairs={{0,0},{1,8},{2,16},{3,24},{4,4},{5,12},{6,20},{7,28},{8,1},{9,9},{... | collective-permute-start | bytes 614408 | tf_op jit(solution)/shard_map/send16/ppermute | solution.py:323
  114.2 18.6 %collective-permute-start.17 = (f32[80,640]{1,0:T(8,128)S(1)}, f32[80,640]{1,0:T(8,128)S(1)}, u32[]{:S(2)}, u32[]{:S(2)}) collective-permute-start(f32[80,640]{1,0:T(8,128)S(1)} %get-tuple-element.85), channel_id=1, source_target_pairs={{0,4},{1,12},{2,20},{3,28},{4,0},{5,8},{6,16},{7,24},{8,5},{9,13},... | collective-permute-start | bytes 614408 | tf_op jit(solution)/shard_map/send17/ppermute | solution.py:323
  132.8 1.0 copy-start.6
  133.8 1.0 copy-start.8
